TPU v7x, 512 devices: a whole 4x8x8 slice. The times are simulated.
512 devices in a mesh: seq: 128 (over z, y, core), tp: 4 (over x).
Axes of the slice: x: 4, y: 8, z: 8, core: 2. Of those that a mesh axis runs over, the one named last changes fastest.
Arguments:
- state: bfloat16 [16384, 1024], P('seq', 'tp'), may hold values from -16 to 16
- cotangent: float32 [16384, 1024], P('seq', 'tp'), may hold values from -40 to 40
- norm_gain: float32 [1024], replicated, may hold values from 0.5 to 1.5
- w_query: bfloat16 [1024, 1024], P(None, 'tp'), may hold values from -8 to 8
- w_key: bfloat16 [1024, 1024], P(None, 'tp'), may hold values from -1 to 1
- w_value: bfloat16 [1024, 1024], P(None, 'tp'), may hold values from -0.1875 to 0.1875
- w_out: bfloat16 [1024, 1024], P('tp'), may hold values from -1.5 to 1.5
Outputs:
- adjoint: float32 [16384, 1024], P('seq', 'tp')
- residual: float32 [16384, 1024], P('seq', 'tp')
All inputs are finite; a program needn't handle non-finite values.
Results may differ from a plain program's by a relative error of at most 0.025.
The roundings to bfloat16 on the way count: a program that leaves them out, or rounds other values in their place, can miss the bound.
Values may be sent and summed in bfloat16 or wider, within the bound.
A program may use at most 64 MiB of HBM per device.

v0:
```python
import math

import jax
import jax.numpy as jnp
from jax import lax
from jax.sharding import Mesh
from jax.sharding import PartitionSpec as P

HD = 128
WIN = 1024
SSTEP = 4
SEQ = ("seq_0", "seq_1", "seq_2")
SEQ_TP = ("seq_0", "seq_1", "seq_2", "tp")


EPSILON = 1e-05


def from_everyone(array, axis):
    copies = jnp.broadcast_to(array, (lax.axis_size(axis), *array.shape))
    return lax.all_to_all(copies, axis, split_axis=0, concat_axis=0, tiled=True)


def in_order(parts, dim):
    dims = list(parts.shape[1:])
    dims[dim] *= parts.shape[0]
    return jnp.moveaxis(parts, 0, dim).reshape(dims)


def collect(array, axis, dim):
    parts = from_everyone(array, axis)
    return in_order(parts, dim)


def shifted(array, axis, by):
    length = lax.axis_size(axis)
    pairs = [(i, i + by) for i in range(length) if 0 <= i + by < length]
    return lax.ppermute(array, axis, pairs)


def cut_along(array, dim, length):
    before, after = (array.shape[:dim], array.shape[dim + 1 :])
    return jnp.moveaxis(array.reshape(*before, length, -1, *after), dim, 0)


def summed_on_arrival(array, axis, dim):
    parts = cut_along(array, dim, lax.axis_size(axis))
    arrived = lax.all_to_all(parts, axis, split_axis=0, concat_axis=0, tiled=True)
    return arrived.sum(axis=0)


def over_axes(array, axes):
    for axis in axes:
        array = lax.psum(array, axis)
    return array


def lower_solve(factor, values):
    result = []
    for index_i in range(values.shape[0]):
        running = values[index_i]
        for index_j in range(index_i):
            running = running - factor[index_i, index_j] * result[index_j]
        result.append(running / factor[index_i, index_i])
    return jnp.stack(result)


def upper_solve(factor, values):
    length_n = values.shape[0]
    result = [None] * length_n
    for index_i in range(length_n - 1, -1, -1):
        running = values[index_i]
        for index_j in range(index_i + 1, length_n):
            running = running - factor[index_j, index_i] * result[index_j]
        result[index_i] = running / factor[index_i, index_i]
    return jnp.stack(result)


def combine_coefficients(gram_matrix, right_side):
    factor = jnp.linalg.cholesky(gram_matrix)
    return upper_solve(factor, lower_solve(factor, right_side))


def on_device(state, cotangent, norm_gain, w_query, w_key, w_value, w_out):
    tok_rows = state.shape[0]
    cols_local = state.shape[1]
    attn_width = w_query.shape[1]
    heads_local = attn_width // HD
    half_span = WIN // 2
    edge_rows = min(tok_rows, half_span)
    reach_count = (half_span + tok_rows - 1) // tok_rows
    key_count = tok_rows + 2 * half_span
    total_rows = tok_rows * lax.axis_size(SEQ)
    first_row = lax.axis_index(SEQ) * tok_rows
    scale_factor = 1.0 / math.sqrt(HD)
    gain_local = lax.dynamic_slice_in_dim(
        norm_gain, lax.axis_index("tp") * cols_local, cols_local, 0
    )
    contract_last = (((1,), (1,)), ((), ()))
    full_state = collect(state, "tp", 1)
    state_full = full_state.astype(jnp.float32)
    inverse = lax.rsqrt(jnp.mean(state_full * state_full, axis=1, keepdims=True) + EPSILON)
    normed = (state_full * inverse * norm_gain[None, :]).astype(jnp.bfloat16)
    w_inputs = jnp.concatenate([w_query, w_key, w_value], axis=1)
    projected = jnp.dot(normed, w_inputs, preferred_element_type=jnp.float32).astype(jnp.bfloat16)
    queries = projected[:, :attn_width].reshape(tok_rows, heads_local, HD)
    key_vecs = projected[:, attn_width : 2 * attn_width].reshape(tok_rows, heads_local, HD)
    values = projected[:, 2 * attn_width :].reshape(tok_rows, heads_local, HD)
    left_parts = []
    for offset in range(reach_count, 0, -1):
        left_parts.append(shifted((key_vecs, values), SEQ, offset))
    right_parts = []
    for offset in range(1, reach_count + 1):
        right_parts.append(shifted((key_vecs, values), SEQ, -offset))
    keys_all = jnp.concatenate(
        [received[0] for received in left_parts]
        + [key_vecs]
        + [received[0] for received in right_parts],
        axis=0,
    )
    values_all = jnp.concatenate(
        [received[1] for received in left_parts]
        + [values]
        + [received[1] for received in right_parts],
        axis=0,
    )
    query_pos = first_row + jnp.arange(tok_rows, dtype=jnp.int32)
    key_pos = first_row - half_span + jnp.arange(key_count, dtype=jnp.int32)
    distance = jnp.abs(key_pos[None, :] - query_pos[:, None])
    valid = ((distance <= half_span) & (key_pos[None, :] >= 0) & (key_pos[None, :] < total_rows))[
        None
    ]
    scores = (
        jnp.einsum("rhe,khe->hrk", queries, keys_all, preferred_element_type=jnp.float32)
        * scale_factor
    )
    row_peak = jnp.max(jnp.where(valid, scores, -jnp.inf), axis=2, keepdims=True)
    raw_weights = jnp.where(valid, jnp.exp(scores - row_peak), 0.0)
    row_total = jnp.sum(raw_weights, axis=2, keepdims=True)
    attn_probs = raw_weights / row_total
    probs_low = attn_probs.astype(jnp.bfloat16)
    attended = jnp.einsum("hrk,khe->rhe", probs_low, values_all, preferred_element_type=jnp.float32)
    krylov = [cotangent]
    differences = []
    for index_n in range(SSTEP):
        whole_vec = collect(krylov[-1].astype(jnp.bfloat16), "tp", 1)
        grad_out = (
            lax.dot_general(whole_vec, w_out, contract_last, preferred_element_type=jnp.float32)
            .astype(jnp.bfloat16)
            .reshape(tok_rows, heads_local, HD)
        )
        row_corr = jnp.sum(grad_out.astype(jnp.float32) * attended, axis=2).T
        grad_prob = jnp.einsum(
            "rhe,khe->hrk", grad_out, values_all, preferred_element_type=jnp.float32
        )
        grad_score = (scale_factor * attn_probs * (grad_prob - row_corr[:, :, None])).astype(
            jnp.bfloat16
        )
        grad_query = jnp.einsum(
            "hrk,khe->rhe", grad_score, keys_all, preferred_element_type=jnp.float32
        ).astype(jnp.bfloat16)
        key_partial = jnp.einsum(
            "hrk,rhe->khe", grad_score, queries, preferred_element_type=jnp.float32
        )
        value_partial = jnp.einsum(
            "hrk,rhe->khe", probs_low, grad_out, preferred_element_type=jnp.float32
        )
        own_key = key_partial[half_span : half_span + tok_rows]
        own_value = value_partial[half_span : half_span + tok_rows]
        for cell_offset in range(1, reach_count + 1):
            lower_row = (reach_count - cell_offset) * edge_rows
            incoming = shifted(
                (
                    key_partial[lower_row : lower_row + edge_rows],
                    value_partial[lower_row : lower_row + edge_rows],
                ),
                SEQ,
                -cell_offset,
            )
            own_key = own_key.at[tok_rows - edge_rows :].add(incoming[0])
            own_value = own_value.at[tok_rows - edge_rows :].add(incoming[1])
        for cell_offset in range(1, reach_count + 1):
            upper_row = half_span + tok_rows + (cell_offset - 1) * edge_rows
            incoming = shifted(
                (
                    key_partial[upper_row : upper_row + edge_rows],
                    value_partial[upper_row : upper_row + edge_rows],
                ),
                SEQ,
                cell_offset,
            )
            own_key = own_key.at[:edge_rows].add(incoming[0])
            own_value = own_value.at[:edge_rows].add(incoming[1])
        grad_key = own_key.astype(jnp.bfloat16)
        grad_value = own_value.astype(jnp.bfloat16)
        stacked = jnp.concatenate(
            [
                grad_query.reshape(tok_rows, attn_width),
                grad_key.reshape(tok_rows, attn_width),
                grad_value.reshape(tok_rows, attn_width),
            ],
            axis=1,
        )
        partial_sum = lax.dot_general(
            stacked, w_inputs, contract_last, preferred_element_type=jnp.float32
        )
        summed = summed_on_arrival(partial_sum, "tp", 1)
        krylov.append(inverse * (gain_local[None, :] * summed))
        differences.append(krylov[index_n] - krylov[index_n + 1])
    diff_stack = jnp.stack(differences)
    local_gram = jnp.einsum("arc,brc->ab", diff_stack, diff_stack, precision=lax.Precision.HIGHEST)
    local_right = jnp.einsum("arc,rc->a", diff_stack, cotangent, precision=lax.Precision.HIGHEST)
    gram_matrix, right_side = (over_axes(local_gram, SEQ_TP), over_axes(local_right, SEQ_TP))
    coefficients = combine_coefficients(gram_matrix, right_side)
    adjoint = coefficients[0] * krylov[0]
    residual = cotangent - coefficients[0] * differences[0]
    for index_n in range(1, SSTEP):
        adjoint = adjoint + coefficients[index_n] * krylov[index_n]
        residual = residual - coefficients[index_n] * differences[index_n]
    return (adjoint, residual)


def solution(mesh):
    split = Mesh(mesh.devices.reshape(8, 8, 2, mesh.shape["tp"]), ("seq_0", "seq_1", "seq_2", "tp"))
    in_specs = (
        P(SEQ, "tp"),
        P(SEQ, "tp"),
        P(),
        P(None, "tp"),
        P(None, "tp"),
        P(None, "tp"),
        P("tp", None),
    )
    out_specs = (P(SEQ, "tp"), P(SEQ, "tp"))
    return jax.shard_map(
        on_device, mesh=split, in_specs=in_specs, out_specs=out_specs, check_vma=False
    )
```

profile of v0, /device:TPU:1, one launch (start us, length us, event | category | flops | bytes accessed | tf_op | source)
XLA Modules:
  0.0 516.8 jit_solution(13610098258207322927)
XLA Ops:
  22.1 7.7 %collective-permute-start.1 = (bf16[128,2,128]{2,0,1:T(8,128)(2,1)S(1)}, bf16[128,2,128]{2,0,1:T(8,128)(2,1)S(1)}, u32[]{:S(2)}, u32[]{:S(2)}) collective-permute-start(bf16[128,2,128]{2,0,1:T(8,128)(2,1)S(1)} %bitcast.236), channel_id=1, source_target_pairs={{0,12},{4,16},{8,20},{12,24},{16,28},{20,32},{24,36},{28,40},{32,4... | collective-permute-start | bytes 196616 | tf_op jit(solution)/shard_map/ppermute | solution.py:38
  43.0 6.2 %collective-permute-start.8 = (bf16[128,2,128]{2,0,1:T(8,128)(2,1)}, bf16[128,2,128]{2,0,1:T(8,128)(2,1)S(1)}, u32[]{:S(2)}, u32[]{:S(2)}) collective-permute-start(bf16[128,2,128]{2,0,1:T(8,128)(2,1)} %bitcast.190), channel_id=1, source_target_pairs={{0,16},{4,20},{8,24},{12,28},{16,32},{20,36},{24,40},{28,44},{32,4... | collective-permute-start | bytes 196616 | tf_op jit(solution)/shard_map/ppermute | solution.py:38
  49.3 6.3 %collective-permute-start.9 = (bf16[128,2,128]{2,0,1:T(8,128)(2,1)}, bf16[128,2,128]{2,0,1:T(8,128)(2,1)S(1)}, u32[]{:S(2)}, u32[]{:S(2)}) collective-permute-start(bf16[128,2,128]{2,0,1:T(8,128)(2,1)} %bitcast.190), channel_id=1, source_target_pairs={{0,12},{4,16},{8,20},{12,24},{16,28},{20,32},{24,36},{28,40},{32,4... | collective-permute-start | bytes 196616 | tf_op jit(solution)/shard_map/ppermute | solution.py:38
  98.7 5.9 %collective-permute-start.23 = (f32[128,2,128]{0,2,1:T(8,128)S(1)}, f32[128,2,128]{0,2,1:T(8,128)S(1)}, u32[]{:S(2)}, u32[]{:S(2)}) collective-permute-start(f32[128,2,128]{0,2,1:T(8,128)S(1)} %get-tuple-element.1345), channel_id=1, source_target_pairs={{0,16},{4,20},{8,24},{12,28},{16,32},{20,36},{24,40},{28,44},{32,4... | collective-permute-start | bytes 393224 | tf_op jit(solution)/shard_map/ppermute | solution.py:38
  125.9 5.9 %collective-permute-start.31 = (f32[128,2,128]{0,2,1:T(8,128)S(1)}, f32[128,2,128]{0,2,1:T(8,128)S(1)}, u32[]{:S(2)}, u32[]{:S(2)}) collective-permute-start(f32[128,2,128]{0,2,1:T(8,128)S(1)} %get-tuple-element.1353), channel_id=1, source_target_pairs={{0,16},{4,20},{8,24},{12,28},{16,32},{20,36},{24,40},{28,44},{32,4... | collective-permute-start | bytes 393224 | tf_op jit(solution)/shard_map/ppermute | solution.py:38
  153.2 7.9 %all_to_all.45 = bf16[4,128,256]{1,2,0:T(8,128)(2,1)S(1)} all-to-all(bf16[4,128,256]{1,2,0:T(8,128)(2,1)S(1)} %broadcast_in_dim.55), channel_id=1, replica_groups=mesh['seq_0'=8,'seq_1'=8,'seq_2'=2,'tp'=4] {'tp'}, dimensions={0} | all-to-all | bytes 524288 | tf_op jit(solution)/shard_map/all_to_all | solution.py:21
  165.3 6.1 %collective-permute-start.32 = (f32[128,2,128]{0,2,1:T(8,128)S(1)}, f32[128,2,128]{0,2,1:T(8,128)S(1)}, u32[]{:S(2)}, u32[]{:S(2)}) collective-permute-start(f32[128,2,128]{0,2,1:T(8,128)S(1)} %get-tuple-element.1328), channel_id=1, source_target_pairs={{4,0},{8,4},{12,8},{16,12},{20,16},{24,20},{28,24},{32,28},{36,32}... | collective-permute-start | bytes 393224 | tf_op jit(solution)/shard_map/ppermute | solution.py:38
  175.6 7.1 %collective-permute-start.36 = (f32[128,2,128]{0,2,1:T(8,128)S(1)}, f32[128,2,128]{0,2,1:T(8,128)S(1)}, u32[]{:S(2)}, u32[]{:S(2)}) collective-permute-start(f32[128,2,128]{0,2,1:T(8,128)S(1)} %get-tuple-element.1332), channel_id=1, source_target_pairs={{0,4},{4,8},{8,12},{12,16},{16,20},{20,24},{24,28},{28,32},{32,36}... | collective-permute-start | bytes 393224 | tf_op jit(solution)/shard_map/ppermute | solution.py:38
  191.9 5.9 %collective-permute-start.39 = (f32[128,2,128]{0,2,1:T(8,128)S(1)}, f32[128,2,128]{0,2,1:T(8,128)S(1)}, u32[]{:S(2)}, u32[]{:S(2)}) collective-permute-start(f32[128,2,128]{0,2,1:T(8,128)S(1)} %get-tuple-element.1329), channel_id=1, source_target_pairs={{0,16},{4,20},{8,24},{12,28},{16,32},{20,36},{24,40},{28,44},{32,4... | collective-permute-start | bytes 393224 | tf_op jit(solution)/shard_map/ppermute | solution.py:38
  218.9 5.9 %collective-permute-start.47 = (f32[128,2,128]{0,2,1:T(8,128)S(1)}, f32[128,2,128]{0,2,1:T(8,128)S(1)}, u32[]{:S(2)}, u32[]{:S(2)}) collective-permute-start(f32[128,2,128]{0,2,1:T(8,128)S(1)} %get-tuple-element.1337), channel_id=1, source_target_pairs={{0,16},{4,20},{8,24},{12,28},{16,32},{20,36},{24,40},{28,44},{32,4... | collective-permute-start | bytes 393224 | tf_op jit(solution)/shard_map/ppermute | solution.py:38
  228.4 11.0 %all_to_all.46 = f32[4,128,256]{2,1,0:T(8,128)} all-to-all(f32[4,128,256]{2,1,0:T(8,128)S(1)} %bitcast.198), channel_id=1, replica_groups=mesh['seq_0'=8,'seq_1'=8,'seq_2'=2,'tp'=4] {'tp'}, dimensions={0} | all-to-all | bytes 1048576 | tf_op jit(solution)/shard_map/all_to_all | solution.py:48
  243.8 7.9 %all_to_all.47 = bf16[4,128,256]{1,2,0:T(8,128)(2,1)S(1)} all-to-all(bf16[4,128,256]{1,2,0:T(8,128)(2,1)S(1)} %broadcast_in_dim.56), channel_id=1, replica_groups=mesh['seq_0'=8,'seq_1'=8,'seq_2'=2,'tp'=4] {'tp'}, dimensions={0} | all-to-all | bytes 524288 | tf_op jit(solution)/shard_map/all_to_all | solution.py:21
  265.7 6.9 %collective-permute-start.52 = (f32[128,2,128]{0,2,1:T(8,128)S(1)}, f32[128,2,128]{0,2,1:T(8,128)S(1)}, u32[]{:S(2)}, u32[]{:S(2)}) collective-permute-start(f32[128,2,128]{0,2,1:T(8,128)S(1)} %get-tuple-element.1316), channel_id=1, source_target_pairs={{0,4},{4,8},{8,12},{12,16},{16,20},{20,24},{24,28},{28,32},{32,36}... | collective-permute-start | bytes 393224 | tf_op jit(solution)/shard_map/ppermute | solution.py:38
  281.8 5.9 %collective-permute-start.55 = (f32[128,2,128]{0,2,1:T(8,128)S(1)}, f32[128,2,128]{0,2,1:T(8,128)S(1)}, u32[]{:S(2)}, u32[]{:S(2)}) collective-permute-start(f32[128,2,128]{0,2,1:T(8,128)S(1)} %get-tuple-element.1313), channel_id=1, source_target_pairs={{0,16},{4,20},{8,24},{12,28},{16,32},{20,36},{24,40},{28,44},{32,4... | collective-permute-start | bytes 393224 | tf_op jit(solution)/shard_map/ppermute | solution.py:38
  308.8 5.9 %collective-permute-start.63 = (f32[128,2,128]{0,2,1:T(8,128)S(1)}, f32[128,2,128]{0,2,1:T(8,128)S(1)}, u32[]{:S(2)}, u32[]{:S(2)}) collective-permute-start(f32[128,2,128]{0,2,1:T(8,128)S(1)} %get-tuple-element.1321), channel_id=1, source_target_pairs={{0,16},{4,20},{8,24},{12,28},{16,32},{20,36},{24,40},{28,44},{32,4... | collective-permute-start | bytes 393224 | tf_op jit(solution)/shard_map/ppermute | solution.py:38
  318.1 11.4 %all_to_all.48 = f32[4,128,256]{2,1,0:T(8,128)} all-to-all(f32[4,128,256]{2,1,0:T(8,128)S(1)} %bitcast.199), channel_id=1, replica_groups=mesh['seq_0'=8,'seq_1'=8,'seq_2'=2,'tp'=4] {'tp'}, dimensions={0} | all-to-all | bytes 1048576 | tf_op jit(solution)/shard_map/all_to_all | solution.py:48
  334.0 7.9 %all_to_all.49 = bf16[4,128,256]{1,2,0:T(8,128)(2,1)S(1)} all-to-all(bf16[4,128,256]{1,2,0:T(8,128)(2,1)S(1)} %broadcast_in_dim.57), channel_id=1, replica_groups=mesh['seq_0'=8,'seq_1'=8,'seq_2'=2,'tp'=4] {'tp'}, dimensions={0} | all-to-all | bytes 524288 | tf_op jit(solution)/shard_map/all_to_all | solution.py:21
  355.5 7.1 %collective-permute-start.68 = (f32[128,2,128]{0,2,1:T(8,128)S(1)}, f32[128,2,128]{0,2,1:T(8,128)S(1)}, u32[]{:S(2)}, u32[]{:S(2)}) collective-permute-start(f32[128,2,128]{0,2,1:T(8,128)S(1)} %get-tuple-element.1300), channel_id=1, source_target_pairs={{0,4},{4,8},{8,12},{12,16},{16,20},{20,24},{24,28},{28,32},{32,36}... | collective-permute-start | bytes 393224 | tf_op jit(solution)/shard_map/ppermute | solution.py:38
  398.9 5.9 %collective-permute-start.79 = (f32[128,2,128]{0,2,1:T(8,128)S(1)}, f32[128,2,128]{0,2,1:T(8,128)S(1)}, u32[]{:S(2)}, u32[]{:S(2)}) collective-permute-start(f32[128,2,128]{0,2,1:T(8,128)S(1)} %get-tuple-element.1305), channel_id=1, source_target_pairs={{0,16},{4,20},{8,24},{12,28},{16,32},{20,36},{24,40},{28,44},{32,4... | collective-permute-start | bytes 393224 | tf_op jit(solution)/shard_map/ppermute | solution.py:38
  412.8 7.8 %all-to-all-done.8 = f32[4,128,256]{2,1,0:T(8,128)S(1)} async-done(((f32[4,128,256]{2,1,0:T(8,128)}), f32[4,128,256]{2,1,0:T(8,128)S(1)}, u32[]{:S(2)}, u32[]{:S(2)}) %all-to-all-start.8) | async-done | bytes 524320 | tf_op jit(solution)/shard_map/all_to_all | solution.py:48
  426.1 38.2 %all-reduce.1 = (f32[4]{0:T(128)S(1)}, f32[4,4]{0,1:T(4,128)S(1)}) all-reduce(f32[4]{0:T(128)S(1)} %convolution_bitcast_fusion.10, f32[4,4]{0,1:T(4,128)S(1)} %convolution_bitcast_fusion.9), channel_id=1, replica_groups=mesh['seq_0'=8,'seq_1'=8,'seq_2'=2,'tp'=4] {'seq_0'}, use_global_device_ids=true, to_apply=%region_11.12 | all-reduce | flops 20 | bytes 160 | tf_op jit(solution)/shard_map/psum | solution.py:54
  464.3 14.4 %all-reduce = (f32[4]{0:T(128)S(1)}, f32[4,4]{0,1:T(4,128)S(1)}) all-reduce(f32[4]{0:T(128)S(1)} %get-tuple-element.1290, f32[4,4]{0,1:T(4,128)S(1)} %get-tuple-element.1291), channel_id=1, replica_groups=mesh['seq_0'=8,'seq_1'=8,'seq_2'=2,'tp'=4] {'seq_1'}, use_global_device_ids=true, to_apply=%region_12.13 | all-reduce | flops 20 | bytes 160 | tf_op jit(solution)/shard_map/psum | solution.py:54
  478.6 11.1 %all-reduce.3 = (f32[4]{0:T(128)S(1)}, f32[4,4]{0,1:T(4,128)S(1)}) all-reduce(f32[4]{0:T(128)S(1)} %get-tuple-element.1288, f32[4,4]{0,1:T(4,128)S(1)} %get-tuple-element.1289), channel_id=1, replica_groups=mesh['seq_0'=8,'seq_1'=8,'seq_2'=2,'tp'=4] {'seq_2'}, use_global_device_ids=true, to_apply=%region_13.14 | all-reduce | flops 20 | bytes 160 | tf_op jit(solution)/shard_map/psum | solution.py:54
  489.8 6.8 %all-reduce.2 = (f32[4]{0:T(128)S(1)}, f32[4,4]{0,1:T(4,128)S(1)}) all-reduce(f32[4]{0:T(128)S(1)} %get-tuple-element.1294, f32[4,4]{0,1:T(4,128)S(1)} %get-tuple-element.1295), channel_id=1, replica_groups=mesh['seq_0'=8,'seq_1'=8,'seq_2'=2,'tp'=4] {'tp'}, use_global_device_ids=true, to_apply=%region_14.15 | all-reduce | flops 20 | bytes 160 | tf_op jit(solution)/shard_map/psum | solution.py:54
  (303 shorter events, 285.5 us)
Async XLA Ops:
  13.6 23.4 %all-to-all-start.1 = ((bf16[4,128,256]{1,2,0:T(8,128)(2,1)}), bf16[4,128,256]{1,2,0:T(8,128)(2,1)S(1)}, u32[]{:S(2)}, u32[]{:S(2)}) async-start(bf16[4,128,256]{1,2,0:T(8,128)(2,1)} %broadcast_in_dim.54), calls=%async_computation.1 | async-start | bytes 524288 | tf_op jit(solution)/shard_map/all_to_all | solution.py:21
  17.8 20.4 %collective-permute-start = (bf16[128,2,128]{2,0,1:T(8,128)(2,1)S(1)}, bf16[128,2,128]{2,0,1:T(8,128)(2,1)S(1)}, u32[]{:S(2)}, u32[]{:S(2)}) collective-permute-start(bf16[128,2,128]{2,0,1:T(8,128)(2,1)S(1)} %bitcast.235), channel_id=1, source_target_pairs={{0,16},{4,20},{8,24},{12,28},{16,32},{20,36},{24,40},{28,44},{32,4... | collective-permute-start | bytes 196616 | tf_op jit(solution)/shard_map/ppermute | solution.py:38
  39.5 19.4 %collective-permute-start.6 = (bf16[128,2,128]{2,0,1:T(8,128)(2,1)S(1)}, bf16[128,2,128]{2,0,1:T(8,128)(2,1)S(1)}, u32[]{:S(2)}, u32[]{:S(2)}) collective-permute-start(bf16[128,2,128]{2,0,1:T(8,128)(2,1)S(1)} %bitcast.241), channel_id=1, source_target_pairs={{12,0},{16,4},{20,8},{24,12},{28,16},{32,20},{36,24},{40,28},{44,3... | collective-permute-start | bytes 196616 | tf_op jit(solution)/shard_map/ppermute | solution.py:38
  40.9 20.4 %collective-permute-start.7 = (bf16[128,2,128]{2,0,1:T(8,128)(2,1)S(1)}, bf16[128,2,128]{2,0,1:T(8,128)(2,1)S(1)}, u32[]{:S(2)}, u32[]{:S(2)}) collective-permute-start(bf16[128,2,128]{2,0,1:T(8,128)(2,1)S(1)} %bitcast.242), channel_id=1, source_target_pairs={{16,0},{20,4},{24,8},{28,12},{32,16},{36,20},{40,24},{44,28},{48,3... | collective-permute-start | bytes 196616 | tf_op jit(solution)/shard_map/ppermute | solution.py:38
  43.0 21.4 %collective-permute-start.8 = (bf16[128,2,128]{2,0,1:T(8,128)(2,1)}, bf16[128,2,128]{2,0,1:T(8,128)(2,1)S(1)}, u32[]{:S(2)}, u32[]{:S(2)}) collective-permute-start(bf16[128,2,128]{2,0,1:T(8,128)(2,1)} %bitcast.190), channel_id=1, source_target_pairs={{0,16},{4,20},{8,24},{12,28},{16,32},{20,36},{24,40},{28,44},{32,4... | collective-permute-start | bytes 196616 | tf_op jit(solution)/shard_map/ppermute | solution.py:38
  83.3 21.3 %collective-permute-start.19 = (f32[128,2,128]{0,2,1:T(8,128)S(1)}, f32[128,2,128]{0,2,1:T(8,128)S(1)}, u32[]{:S(2)}, u32[]{:S(2)}) collective-permute-start(f32[128,2,128]{0,2,1:T(8,128)S(1)} %get-tuple-element.1349), channel_id=1, source_target_pairs={{16,0},{20,4},{24,8},{28,12},{32,16},{36,20},{40,24},{44,28},{48,3... | collective-permute-start | bytes 393224 | tf_op jit(solution)/shard_map/ppermute | solution.py:38
  84.6 22.1 %collective-permute-start.20 = (f32[128,2,128]{0,2,1:T(8,128)S(1)}, f32[128,2,128]{0,2,1:T(8,128)S(1)}, u32[]{:S(2)}, u32[]{:S(2)}) collective-permute-start(f32[128,2,128]{0,2,1:T(8,128)S(1)} %get-tuple-element.1348), channel_id=1, source_target_pairs={{0,4},{4,8},{8,12},{12,16},{16,20},{20,24},{24,28},{28,32},{32,36}... | collective-permute-start | bytes 393224 | tf_op jit(solution)/shard_map/ppermute | solution.py:38
  88.6 19.4 %collective-permute-start.21 = (f32[128,2,128]{0,2,1:T(8,128)S(1)}, f32[128,2,128]{0,2,1:T(8,128)S(1)}, u32[]{:S(2)}, u32[]{:S(2)}) collective-permute-start(f32[128,2,128]{0,2,1:T(8,128)S(1)} %get-tuple-element.1347), channel_id=1, source_target_pairs={{0,8},{4,12},{8,16},{12,20},{16,24},{20,28},{24,32},{28,36},{32,40... | collective-permute-start | bytes 393224 | tf_op jit(solution)/shard_map/ppermute | solution.py:38
  109.7 22.2 %collective-permute-start.27 = (f32[128,2,128]{0,2,1:T(8,128)S(1)}, f32[128,2,128]{0,2,1:T(8,128)S(1)}, u32[]{:S(2)}, u32[]{:S(2)}) collective-permute-start(f32[128,2,128]{0,2,1:T(8,128)S(1)} %get-tuple-element.1357), channel_id=1, source_target_pairs={{16,0},{20,4},{24,8},{28,12},{32,16},{36,20},{40,24},{44,28},{48,3... | collective-permute-start | bytes 393224 | tf_op jit(solution)/shard_map/ppermute | solution.py:38
  111.0 20.9 %collective-permute-start.28 = (f32[128,2,128]{0,2,1:T(8,128)S(1)}, f32[128,2,128]{0,2,1:T(8,128)S(1)}, u32[]{:S(2)}, u32[]{:S(2)}) collective-permute-start(f32[128,2,128]{0,2,1:T(8,128)S(1)} %get-tuple-element.1356), channel_id=1, source_target_pairs={{0,4},{4,8},{8,12},{12,16},{16,20},{20,24},{24,28},{28,32},{32,36}... | collective-permute-start | bytes 393224 | tf_op jit(solution)/shard_map/ppermute | solution.py:38
  173.0 18.9 %collective-permute-start.34 = (f32[128,2,128]{0,2,1:T(8,128)S(1)}, f32[128,2,128]{0,2,1:T(8,128)S(1)}, u32[]{:S(2)}, u32[]{:S(2)}) collective-permute-start(f32[128,2,128]{0,2,1:T(8,128)S(1)} %get-tuple-element.1334), channel_id=1, source_target_pairs={{12,0},{16,4},{20,8},{24,12},{28,16},{32,20},{36,24},{40,28},{44,3... | collective-permute-start | bytes 393224 | tf_op jit(solution)/shard_map/ppermute | solution.py:38
  174.3 23.5 %collective-permute-start.35 = (f32[128,2,128]{0,2,1:T(8,128)S(1)}, f32[128,2,128]{0,2,1:T(8,128)S(1)}, u32[]{:S(2)}, u32[]{:S(2)}) collective-permute-start(f32[128,2,128]{0,2,1:T(8,128)S(1)} %get-tuple-element.1333), channel_id=1, source_target_pairs={{16,0},{20,4},{24,8},{28,12},{32,16},{36,20},{40,24},{44,28},{48,3... | collective-permute-start | bytes 393224 | tf_op jit(solution)/shard_map/ppermute | solution.py:38
  175.6 24.2 %collective-permute-start.36 = (f32[128,2,128]{0,2,1:T(8,128)S(1)}, f32[128,2,128]{0,2,1:T(8,128)S(1)}, u32[]{:S(2)}, u32[]{:S(2)}) collective-permute-start(f32[128,2,128]{0,2,1:T(8,128)S(1)} %get-tuple-element.1332), channel_id=1, source_target_pairs={{0,4},{4,8},{8,12},{12,16},{16,20},{20,24},{24,28},{28,32},{32,36}... | collective-permute-start | bytes 393224 | tf_op jit(solution)/shard_map/ppermute | solution.py:38
  202.8 22.1 %collective-permute-start.43 = (f32[128,2,128]{0,2,1:T(8,128)S(1)}, f32[128,2,128]{0,2,1:T(8,128)S(1)}, u32[]{:S(2)}, u32[]{:S(2)}) collective-permute-start(f32[128,2,128]{0,2,1:T(8,128)S(1)} %get-tuple-element.1341), channel_id=1, source_target_pairs={{16,0},{20,4},{24,8},{28,12},{32,16},{36,20},{40,24},{44,28},{48,3... | collective-permute-start | bytes 393224 | tf_op jit(solution)/shard_map/ppermute | solution.py:38
  204.2 20.8 %collective-permute-start.44 = (f32[128,2,128]{0,2,1:T(8,128)S(1)}, f32[128,2,128]{0,2,1:T(8,128)S(1)}, u32[]{:S(2)}, u32[]{:S(2)}) collective-permute-start(f32[128,2,128]{0,2,1:T(8,128)S(1)} %get-tuple-element.1340), channel_id=1, source_target_pairs={{0,4},{4,8},{8,12},{12,16},{16,20},{20,24},{24,28},{28,32},{32,36}... | collective-permute-start | bytes 393224 | tf_op jit(solution)/shard_map/ppermute | solution.py:38
  264.4 23.3 %collective-permute-start.51 = (f32[128,2,128]{0,2,1:T(8,128)S(1)}, f32[128,2,128]{0,2,1:T(8,128)S(1)}, u32[]{:S(2)}, u32[]{:S(2)}) collective-permute-start(f32[128,2,128]{0,2,1:T(8,128)S(1)} %get-tuple-element.1317), channel_id=1, source_target_pairs={{16,0},{20,4},{24,8},{28,12},{32,16},{36,20},{40,24},{44,28},{48,3... | collective-permute-start | bytes 393224 | tf_op jit(solution)/shard_map/ppermute | solution.py:38
  265.7 24.0 %collective-permute-start.52 = (f32[128,2,128]{0,2,1:T(8,128)S(1)}, f32[128,2,128]{0,2,1:T(8,128)S(1)}, u32[]{:S(2)}, u32[]{:S(2)}) collective-permute-start(f32[128,2,128]{0,2,1:T(8,128)S(1)} %get-tuple-element.1316), channel_id=1, source_target_pairs={{0,4},{4,8},{8,12},{12,16},{16,20},{20,24},{24,28},{28,32},{32,36}... | collective-permute-start | bytes 393224 | tf_op jit(solution)/shard_map/ppermute | solution.py:38
  292.8 22.1 %collective-permute-start.59 = (f32[128,2,128]{0,2,1:T(8,128)S(1)}, f32[128,2,128]{0,2,1:T(8,128)S(1)}, u32[]{:S(2)}, u32[]{:S(2)}) collective-permute-start(f32[128,2,128]{0,2,1:T(8,128)S(1)} %get-tuple-element.1325), channel_id=1, source_target_pairs={{16,0},{20,4},{24,8},{28,12},{32,16},{36,20},{40,24},{44,28},{48,3... | collective-permute-start | bytes 393224 | tf_op jit(solution)/shard_map/ppermute | solution.py:38
  294.1 20.8 %collective-permute-start.60 = (f32[128,2,128]{0,2,1:T(8,128)S(1)}, f32[128,2,128]{0,2,1:T(8,128)S(1)}, u32[]{:S(2)}, u32[]{:S(2)}) collective-permute-start(f32[128,2,128]{0,2,1:T(8,128)S(1)} %get-tuple-element.1324), channel_id=1, source_target_pairs={{0,4},{4,8},{8,12},{12,16},{16,20},{20,24},{24,28},{28,32},{32,36}... | collective-permute-start | bytes 393224 | tf_op jit(solution)/shard_map/ppermute | solution.py:38
  352.9 18.8 %collective-permute-start.66 = (f32[128,2,128]{0,2,1:T(8,128)S(1)}, f32[128,2,128]{0,2,1:T(8,128)S(1)}, u32[]{:S(2)}, u32[]{:S(2)}) collective-permute-start(f32[128,2,128]{0,2,1:T(8,128)S(1)} %get-tuple-element.1302), channel_id=1, source_target_pairs={{12,0},{16,4},{20,8},{24,12},{28,16},{32,20},{36,24},{40,28},{44,3... | collective-permute-start | bytes 393224 | tf_op jit(solution)/shard_map/ppermute | solution.py:38
  354.2 23.5 %collective-permute-start.67 = (f32[128,2,128]{0,2,1:T(8,128)S(1)}, f32[128,2,128]{0,2,1:T(8,128)S(1)}, u32[]{:S(2)}, u32[]{:S(2)}) collective-permute-start(f32[128,2,128]{0,2,1:T(8,128)S(1)} %get-tuple-element.1301), channel_id=1, source_target_pairs={{16,0},{20,4},{24,8},{28,12},{32,16},{36,20},{40,24},{44,28},{48,3... | collective-permute-start | bytes 393224 | tf_op jit(solution)/shard_map/ppermute | solution.py:38
  355.5 24.2 %collective-permute-start.68 = (f32[128,2,128]{0,2,1:T(8,128)S(1)}, f32[128,2,128]{0,2,1:T(8,128)S(1)}, u32[]{:S(2)}, u32[]{:S(2)}) collective-permute-start(f32[128,2,128]{0,2,1:T(8,128)S(1)} %get-tuple-element.1300), channel_id=1, source_target_pairs={{0,4},{4,8},{8,12},{12,16},{16,20},{20,24},{24,28},{28,32},{32,36}... | collective-permute-start | bytes 393224 | tf_op jit(solution)/shard_map/ppermute | solution.py:38
  382.7 22.2 %collective-permute-start.75 = (f32[128,2,128]{0,2,1:T(8,128)S(1)}, f32[128,2,128]{0,2,1:T(8,128)S(1)}, u32[]{:S(2)}, u32[]{:S(2)}) collective-permute-start(f32[128,2,128]{0,2,1:T(8,128)S(1)} %get-tuple-element.1309), channel_id=1, source_target_pairs={{16,0},{20,4},{24,8},{28,12},{32,16},{36,20},{40,24},{44,28},{48,3... | collective-permute-start | bytes 393224 | tf_op jit(solution)/shard_map/ppermute | solution.py:38
  384.0 20.9 %collective-permute-start.76 = (f32[128,2,128]{0,2,1:T(8,128)S(1)}, f32[128,2,128]{0,2,1:T(8,128)S(1)}, u32[]{:S(2)}, u32[]{:S(2)}) collective-permute-start(f32[128,2,128]{0,2,1:T(8,128)S(1)} %get-tuple-element.1308), channel_id=1, source_target_pairs={{0,4},{4,8},{8,12},{12,16},{16,20},{20,24},{24,28},{28,32},{32,36}... | collective-permute-start | bytes 393224 | tf_op jit(solution)/shard_map/ppermute | solution.py:38
  (73 other events, 1022.6 us)
where the time goes:
time: 521 us; the launch traced here: 517 us
  starting transfers between devices  291 us (56%)
  blocking collectives  117 us (22%)
  waiting for transfers between devices  35.3 us (7%)
  local copies, waits for them, and re-layouts  21.6 us (4%)
  matrix products  21.5 us (4%)
  between operations  17.9 us (3%)
  other arithmetic  13.2 us (3%)
    ppermute x80, starting transfers between devices, shifted(): return lax.ppermute(array, axis, pairs)  274 us
    psum x4, blocking collectives, over_axes(): array = lax.psum(array, axis)  70.5 us
    all_to_all x3, blocking collectives, from_everyone(): return lax.all_to_all(copies, axis, split_axis=0, concat_axis=0, tiled=True)  23.7 us
    all_to_all x2, blocking collectives, summed_on_arrival(): lax.all_to_all(parts, axis, split_axis=0, concat_axis=0, tiled=True)  22.4 us
    ppermute x80, waiting for transfers between devices, shifted(): return lax.ppermute(array, axis, pairs)  17.8 us
    all_to_all x2, waiting for transfers between devices, summed_on_arrival(): lax.all_to_all(parts, axis, split_axis=0, concat_axis=0, tiled=True)  13.6 us
  transfers between devices with their start and end apart: 84, of which 10 were waited for; matrix products, arithmetic and copies ran while one was open for 2% of the time, Pallas kernels for 0%

commit v1 on v0

v1 whole, which is shorter than its diff:
```python
import functools
import math

import jax
import jax.numpy as jnp
from jax import lax
from jax.experimental import pallas as pl
from jax.experimental.pallas import tpu as pltpu
from jax.sharding import PartitionSpec as P

HD = 128
HALF = 512
SSTEP = 4
EPSILON = 1e-05
TOK = 128
CHIP = 2 * TOK
SPAN = CHIP + 2 * HALF
REACH = HALF // CHIP
CHUNKS = 2 * REACH + 1
MSG = TOK + 16
SCALE = 1.0 / math.sqrt(HD)
LOW = -1e30
MESH = pl.DeviceIdType.MESH
F32 = jnp.float32
BF16 = jnp.bfloat16

NT = (((1,), (1,)), ((), ()))
NN = (((1,), (0,)), ((), ()))


def dot(a, b, dims):
    return lax.dot_general(a, b, dims, preferred_element_type=F32)


def wait_for(ref, sem):
    pltpu.make_async_copy(ref, ref, sem).wait()


def kernel(
    sizes,
    state,
    cot,
    gain,
    w_query,
    w_key,
    w_value,
    w_out,
    adj_out,
    res_out,
    w_in,
    w_o,
    gain_v,
    xs,
    xg,
    qkv,
    win,
    att_head,
    att_own,
    stats,
    probs,
    probs_t,
    probs_tb,
    g_msg,
    g_win,
    g_full,
    g_swap,
    rs_send,
    rs_recv,
    kry,
    dif,
    inv_v,
    tiles,
    tile_recv,
    outs,
    sem_load,
    sem_xs_s,
    sem_xs_r,
    sem_xg_s,
    sem_xg_r,
    sem_q_s,
    sem_q_r,
    sem_a_s,
    sem_a_r,
    sem_st_s,
    sem_st_r,
    sem_g_s,
    sem_g_r,
    sem_sw_s,
    sem_sw_r,
    sem_rs_s,
    sem_rs_r,
    sem_t_s,
    sem_t_r,
    sem_out,
):
    n_seq, n_tp, n_y, n_z = sizes
    n_chip = n_seq // 2
    s = lax.axis_index("seq")
    tp = lax.axis_index("tp")
    chip = lax.div(s, 2)
    core = lax.rem(s, 2)
    y = lax.rem(chip, n_y)
    z = lax.div(chip, n_y)
    other = 1 - core
    cols = xs.shape[2]
    pair = (2 * chip + other, tp)

    def at_tp(offset):
        return lax.rem(tp + offset, n_tp)

    def at_chip(offset):
        return lax.rem(chip + offset + n_chip, n_chip)

    tp_far = sorted(range(1, n_tp), key=lambda o: -min(o, n_tp - o))
    halo = [d for k in range(REACH, 0, -1) for d in (-k, k)]
    stage_a = [
        (2 * chip + lax.rem(core + oc, 2), at_tp(ox))
        for ox in range(n_tp)
        for oc in range(2)
        if (ox, oc) != (0, 0)
    ]
    stage_b = [
        (2 * (z * n_y + lax.rem(y + o, n_y)) + core, tp) for o in range(1, n_y)
    ]
    stage_c = [
        (2 * (lax.rem(z + o, n_z) * n_y + y) + core, tp) for o in range(1, n_z)
    ]

    def send(src, dst, ssem, rsem, device):
        pltpu.make_async_remote_copy(
            src_ref=src,
            dst_ref=dst,
            send_sem=ssem,
            recv_sem=rsem,
            device_id=device,
            device_id_type=MESH,
        ).start()

    loads = [
        (state, xs.at[tp]),
        (cot, kry.at[0]),
        (gain, gain_v),
        (w_query, w_in.at[0]),
        (w_key, w_in.at[1]),
        (w_value, w_in.at[2]),
        (w_out, w_o),
    ]
    loading = [
        pltpu.make_async_copy(src, dst, sem_load.at[k])
        for k, (src, dst) in enumerate(loads)
    ]
    for copy in loading:
        copy.start()

    barrier = pltpu.get_barrier_semaphore()
    greeted = stage_a + stage_b + stage_c
    for d in halo:
        for h in range(2):
            greeted.append((2 * at_chip(d) + h, tp))
    for device in greeted:
        pl.semaphore_signal(barrier, inc=1, device_id=device, device_id_type=MESH)
    pl.semaphore_wait(barrier, len(greeted))

    for o in tp_far:
        send(state, xs.at[tp], sem_xs_s, sem_xs_r, (s, at_tp(o)))

    def send_vector(n):
        for o in tp_far:
            send(
                xg.at[n, tp],
                xg.at[n, tp],
                sem_xg_s.at[n],
                sem_xg_r.at[n],
                (s, at_tp(o)),
            )

    loading[1].wait()
    xg[0, tp] = kry[0].astype(BF16)
    send_vector(0)

    loading[0].wait()
    loading[2].wait()
    wait_for(xs.at[pl.ds(0, n_tp - 1)], sem_xs_r)
    total = jnp.zeros((TOK, 1), F32)
    for r in range(n_tp):
        block = xs[r].astype(F32)
        total = total + jnp.sum(block * block, axis=1, keepdims=True)
    inverse = lax.rsqrt(total * (1.0 / (n_tp * cols)) + EPSILON)
    inv_v[...] = jnp.broadcast_to(inverse, inv_v.shape)
    normed = [
        (xs[r].astype(F32) * inverse * gain_v[:, r * cols : (r + 1) * cols]).astype(BF16)
        for r in range(n_tp)
    ]

    own_rows = pl.ds(pl.multiple_of((2 * REACH + core) * TOK, TOK), TOK)

    def slot_rows(d):
        return pl.ds(pl.multiple_of((2 * (REACH - d) + core) * TOK, TOK), TOK)

    for t in (1, 0, 2):
        loading[3 + t].wait()
        acc = jnp.zeros((TOK, 2 * HD), F32)
        for r in range(n_tp):
            acc = acc + dot(normed[r], w_in[t, r * cols : (r + 1) * cols, :], NN)
        acc = acc.astype(BF16)
        for h in range(2):
            qkv[t, h] = acc[:, h * HD : (h + 1) * HD]
        send(
            qkv.at[t, other],
            win.at[t, slot_rows(0)],
            sem_q_s,
            sem_q_r.at[t, REACH],
            pair,
        )
        if t == 1:
            for d in halo:
                for h in range(2):
                    send(
                        qkv.at[t, h],
                        win.at[t, slot_rows(d)],
                        sem_q_s,
                        sem_q_r.at[t, REACH - d],
                        (2 * at_chip(d) + h, tp),
                    )
        win[t, own_rows, :] = qkv[t, core]
    for t in (2, 0):
        for d in halo:
            for h in range(2):
                send(
                    qkv.at[t, h],
                    win.at[t, slot_rows(d)],
                    sem_q_s,
                    sem_q_r.at[t, REACH - d],
                    (2 * at_chip(d) + h, tp),
                )

    def wait_window(t, k):
        rows = TOK if k == REACH else CHIP
        wait_for(win.at[t, pl.ds(0, rows)], sem_q_r.at[t, k])

    arrival = sorted(range(CHUNKS), key=lambda k: abs(k - REACH))
    own = slice(HALF, HALF + CHIP)

    def valid(k):
        row = lax.broadcasted_iota(jnp.int32, (CHIP, CHIP), 0)
        col = lax.broadcasted_iota(jnp.int32, (CHIP, CHIP), 1) + k * CHIP
        place = chip * CHIP - HALF + col
        away = row + HALF - col
        return (
            (away <= HALF)
            & (away >= -HALF)
            & (place >= 0)
            & (place < n_chip * CHIP)
        )

    def part(k):
        return slice(k * CHIP, (k + 1) * CHIP)

    wait_window(0, REACH)
    queries = win[0, own, :]
    peak = jnp.full((CHIP, 1), LOW, F32)
    for k in arrival:
        wait_window(1, k)
        scores = dot(queries, win[1, part(k), :], NT) * SCALE
        scores = jnp.where(valid(k), scores, LOW)
        probs[:, part(k)] = scores
        peak = jnp.maximum(peak, jnp.max(scores, axis=1, keepdims=True))
    mass = jnp.zeros((CHIP, 1), F32)
    for k in arrival:
        raw = jnp.exp(probs[:, part(k)] - peak)
        probs[:, part(k)] = raw
        mass = mass + jnp.sum(raw, axis=1, keepdims=True)
    share = 1.0 / mass
    both = jnp.concatenate(
        [
            jnp.broadcast_to(peak, (CHIP, HD)).T[0:1],
            jnp.broadcast_to(share, (CHIP, HD)).T[0:1],
            jnp.zeros((6, CHIP), F32),
        ],
        axis=0,
    )
    stats[REACH] = both
    for d in halo:
        send(
            stats.at[REACH],
            stats.at[REACH - d],
            sem_st_s,
            sem_st_r,
            (2 * at_chip(d) + core, tp),
        )
    attended = jnp.zeros((CHIP, HD), F32)
    for k in arrival:
        wait_window(2, k)
        weights = probs[:, part(k)] * share
        probs[:, part(k)] = weights * SCALE
        attended = attended + dot(weights.astype(BF16), win[2, part(k), :], NN)
    att_head[...] = attended
    other_half = pl.ds(pl.multiple_of(other * TOK, TOK), TOK)
    own_half = pl.ds(pl.multiple_of(core * TOK, TOK), TOK)
    send(att_head.at[other_half], att_own.at[core], sem_a_s, sem_a_r, pair)
    att_own[core] = att_head[own_half, :]

    def send_grad_out(n):
        wait_for(xg.at[n, pl.ds(0, n_tp - 1)], sem_xg_r.at[n])
        acc = jnp.zeros((TOK, 2 * HD), F32)
        for r in range(n_tp):
            acc = acc + dot(xg[n, r], w_o[:, r * cols : (r + 1) * cols], NT)
        acc = acc.astype(BF16)
        row = lax.broadcasted_iota(jnp.int32, (16, HD), 0)
        for h in range(2):
            grad = acc[:, h * HD : (h + 1) * HD]
            corr = jnp.sum((grad.astype(F32) * att_own[h]).T, axis=0, keepdims=True)
            high = corr.astype(BF16).astype(F32)
            rest = corr - high
            mid = rest.astype(BF16).astype(F32)
            low = rest - mid
            terms = jnp.where(row == 0, high, jnp.where(row == 1, mid, low))
            g_msg[n, h, 0:TOK, :] = grad
            g_msg[n, h, TOK:MSG, :] = terms.astype(BF16)
        send(
            g_msg.at[n, other],
            g_win.at[n, 2 * REACH + core],
            sem_g_s.at[n],
            sem_g_r.at[n, REACH],
            pair,
        )
        for d in halo:
            for h in range(2):
                send(
                    g_msg.at[n, h],
                    g_win.at[n, 2 * (REACH - d) + core],
                    sem_g_s.at[n],
                    sem_g_r.at[n, REACH - d],
                    (2 * at_chip(d) + h, tp),
                )
        g_win[n, 2 * REACH + core] = g_msg[n, core]

    loading[6].wait()
    wait_for(att_own.at[0], sem_a_r)
    send_grad_out(0)

    keys = win[1, own, :]
    values = win[2, own, :]
    wait_for(stats.at[pl.ds(0, CHUNKS - 1)], sem_st_r)
    for k in arrival:
        wait_window(0, k) if k != REACH else None
        scores = dot(keys, win[0, part(k), :], NT) * SCALE
        pair_stats = stats[k]
        scores = jnp.where(valid(k), scores - pair_stats[0:1], LOW)
        weights = jnp.exp(scores) * pair_stats[1:2]
        probs_t[:, part(k)] = weights * SCALE
        probs_tb[:, part(k)] = weights.astype(BF16)

    gain_own = gain_v[:, pl.ds(pl.multiple_of(tp * cols, cols), cols)]

    def product(n, carry):
        def window_grad(k):
            return jnp.concatenate(
                [g_win[n, 2 * k, 0:TOK, :], g_win[n, 2 * k + 1, 0:TOK, :]], axis=0
            )

        def window_corr(k):
            halves = []
            for half in range(2):
                terms = g_win[n, 2 * k + half, TOK:MSG, :].astype(F32)
                halves.append(terms[0:1] + (terms[1:2] + terms[2:3]))
            return jnp.concatenate(halves, axis=1)

        wait_for(g_win.at[n, 0], sem_g_r.at[n, REACH])
        grad = window_grad(REACH)
        corr = jnp.sum(grad.astype(F32) * att_head[...], axis=1, keepdims=True)
        grad_q = jnp.zeros((CHIP, HD), F32)
        for k in range(CHUNKS):
            grad_p = dot(grad, win[2, part(k), :], NT)
            score = (probs[:, part(k)] * (grad_p - corr)).astype(BF16)
            grad_q = grad_q + dot(score, win[1, part(k), :], NN)
        grad_k = jnp.zeros((CHIP, HD), F32)
        grad_v = jnp.zeros((CHIP, HD), F32)
        for k in arrival:
            if k != REACH:
                wait_for(g_win.at[n, pl.ds(0, 2)], sem_g_r.at[n, k])
            grad = window_grad(k)
            grad_p = dot(win[2, own, :], grad, NT)
            score = (probs_t[:, part(k)] * (grad_p - window_corr(k))).astype(BF16)
            grad_k = grad_k + dot(score, win[0, part(k), :], NN)
            grad_v = grad_v + dot(probs_tb[:, part(k)], grad, NN)
        for t, whole in enumerate((grad_q, grad_k, grad_v)):
            whole = whole.astype(BF16)
            first, second = whole[0:TOK], whole[TOK:CHIP]
            mine = core == 0
            g_full[n, core, t] = jnp.where(mine, first, second)
            g_swap[n, t] = jnp.where(mine, second, first)
        send(g_swap.at[n], g_full.at[n, core], sem_sw_s.at[n], sem_sw_r.at[n], pair)
        wait_for(g_swap.at[n], sem_sw_r.at[n])
        grads = [
            jnp.concatenate([g_full[n, 0, t], g_full[n, 1, t]], axis=1) for t in range(3)
        ]

        def partial_sum(o):
            rows = pl.ds(pl.multiple_of(at_tp(o) * cols, cols), cols)
            acc = jnp.zeros((TOK, cols), F32)
            for t in range(3):
                acc = acc + dot(grads[t], w_in[t, rows, :], NT)
            return acc

        for o in tp_far:
            rs_send[n, o - 1] = partial_sum(o).astype(BF16)
            send(
                rs_send.at[n, o - 1],
                rs_recv.at[n, o - 1],
                sem_rs_s.at[n],
                sem_rs_r.at[n],
                (s, at_tp(o)),
            )
        summed = partial_sum(0)
        wait_for(rs_recv.at[n], sem_rs_r.at[n])
        for o in range(1, n_tp):
            summed = summed + rs_recv[n, o - 1].astype(F32)
        vector = inv_v[:, 0:1] * (gain_own * summed)
        kry[n + 1] = vector
        dif[n] = kry[n] - vector

        @pl.when(n < SSTEP - 1)
        def _():
            xg[n + 1, tp] = vector.astype(BF16)
            send_vector(n + 1)
            send_grad_out(n + 1)

        return carry

    lax.fori_loop(0, SSTEP, product, 0)

    tiles[0] = jnp.zeros(tiles.shape[1:], F32)
    place = 0
    where = {}
    for a in range(SSTEP):
        for b in list(range(a + 1)) + ["right"]:
            factor = kry[0] if b == "right" else dif[b]
            row = jnp.sum(dif[a] * factor, axis=0, keepdims=True)
            folded = row[:, 0:HD]
            for start in range(HD, cols, HD):
                folded = folded + row[:, start : start + HD]
            tiles[0, place : place + 1, :] = folded
            where[a, b] = place
            place += 1
    start = 0
    for stage, devices in enumerate((stage_a, stage_b, stage_c)):
        for k, device in enumerate(devices):
            send(
                tiles.at[stage],
                tile_recv.at[start + k],
                sem_t_s,
                sem_t_r.at[stage],
                device,
            )
        wait_for(tile_recv.at[pl.ds(start, len(devices))], sem_t_r.at[stage])
        whole = tiles[stage]
        for k in range(len(devices)):
            whole = whole + tile_recv[start + k]
        tiles[stage + 1] = whole
        start += len(devices)

    def inner(a, b):
        return jnp.sum(
            whole[where[a, b] : where[a, b] + 1], axis=1, keepdims=True
        )

    factor = {}
    for a in range(SSTEP):
        for b in range(a + 1):
            value = inner(a, b)
            for c in range(b):
                value = value - factor[a, c] * factor[b, c]
            factor[a, b] = jnp.sqrt(value) if a == b else value / factor[b, b]
    half = []
    for a in range(SSTEP):
        value = inner(a, "right")
        for b in range(a):
            value = value - factor[a, b] * half[b]
        half.append(value / factor[a, a])
    coef = [None] * SSTEP
    for a in range(SSTEP - 1, -1, -1):
        value = half[a]
        for b in range(a + 1, SSTEP):
            value = value - factor[b, a] * coef[b]
        coef[a] = value / factor[a, a]
    adjoint = coef[0] * kry[0]
    for n in range(1, SSTEP):
        adjoint = adjoint + coef[n] * kry[n]
    outs[0] = adjoint
    out_a = pltpu.make_async_copy(outs.at[0], adj_out, sem_out.at[0])
    out_a.start()
    residual = kry[0]
    for n in range(SSTEP):
        residual = residual - coef[n] * dif[n]
    outs[1] = residual
    out_b = pltpu.make_async_copy(outs.at[1], res_out, sem_out.at[1])
    out_b.start()

    wait_for(xs.at[pl.ds(0, n_tp - 1)], sem_xs_s)
    wait_for(win.at[:, pl.ds(0, (4 * REACH + 1) * TOK)], sem_q_s)
    wait_for(att_own.at[0], sem_a_s)
    wait_for(stats.at[pl.ds(0, CHUNKS - 1)], sem_st_s)
    for n in range(SSTEP):
        wait_for(xg.at[n, pl.ds(0, n_tp - 1)], sem_xg_s.at[n])
        wait_for(g_win.at[n, pl.ds(0, 4 * REACH + 1)], sem_g_s.at[n])
        wait_for(g_swap.at[n], sem_sw_s.at[n])
        wait_for(rs_send.at[n], sem_rs_s.at[n])
    wait_for(tile_recv.at[pl.ds(0, start)], sem_t_s)
    out_a.wait()
    out_b.wait()


def on_device(sizes, state, cotangent, norm_gain, w_query, w_key, w_value, w_out):
    n_seq, n_tp, n_y, n_z = sizes
    tok, cols = state.shape
    width = n_tp * cols
    tile_count = (2 * n_tp - 1) + (n_y - 1) + (n_z - 1)
    dma = pltpu.SemaphoreType.DMA
    scratch = [
        pltpu.VMEM((3, width, 2 * HD), BF16),
        pltpu.VMEM((2 * HD, width), BF16),
        pltpu.VMEM((1, width), F32),
        pltpu.VMEM((n_tp, tok, cols), BF16),
        pltpu.VMEM((SSTEP, n_tp, tok, cols), BF16),
        pltpu.VMEM((3, 2, tok, HD), BF16),
        pltpu.VMEM((3, SPAN, HD), BF16),
        pltpu.VMEM((CHIP, HD), F32),
        pltpu.VMEM((2, tok, HD), F32),
        pltpu.VMEM((CHUNKS, 8, CHIP), F32),
        pltpu.VMEM((CHIP, SPAN), F32),
        pltpu.VMEM((CHIP, SPAN), F32),
        pltpu.VMEM((CHIP, SPAN), BF16),
        pltpu.VMEM((SSTEP, 2, MSG, HD), BF16),
        pltpu.VMEM((SSTEP, 2 * CHUNKS, MSG, HD), BF16),
        pltpu.VMEM((SSTEP, 2, 3, tok, HD), BF16),
        pltpu.VMEM((SSTEP, 3, tok, HD), BF16),
        pltpu.VMEM((SSTEP, n_tp - 1, tok, cols), BF16),
        pltpu.VMEM((SSTEP, n_tp - 1, tok, cols), BF16),
        pltpu.VMEM((SSTEP + 1, tok, cols), F32),
        pltpu.VMEM((SSTEP, tok, cols), F32),
        pltpu.VMEM((tok, HD), F32),
        pltpu.VMEM((4, 16, HD), F32),
        pltpu.VMEM((tile_count, 16, HD), F32),
        pltpu.VMEM((2, tok, cols), F32),
        dma((7,)),
        dma,
        dma,
        dma((SSTEP,)),
        dma((SSTEP,)),
        dma,
        dma((3, CHUNKS)),
        dma,
        dma,
        dma,
        dma,
        dma((SSTEP,)),
        dma((SSTEP, CHUNKS)),
        dma((SSTEP,)),
        dma((SSTEP,)),
        dma((SSTEP,)),
        dma((SSTEP,)),
        dma,
        dma((3,)),
        dma((2,)),
    ]
    anywhere = pl.BlockSpec(memory_space=pl.ANY)
    shape = jax.ShapeDtypeStruct((tok, cols), F32)
    return pl.pallas_call(
        functools.partial(kernel, sizes),
        out_shape=(shape, shape),
        in_specs=[anywhere] * 7,
        out_specs=(anywhere, anywhere),
        scratch_shapes=scratch,
        compiler_params=pltpu.CompilerParams(
            collective_id=0, has_side_effects=True, vmem_limit_bytes=40 * 2**20
        ),
        name="block",
    )(state, cotangent, norm_gain.reshape(1, width), w_query, w_key, w_value, w_out)


def solution(mesh):
    n_seq, n_tp = mesh.shape["seq"], mesh.shape["tp"]
    n_chip = n_seq // 2
    n_y = 1
    while n_y * n_y < n_chip:
        n_y *= 2
    sizes = (n_seq, n_tp, n_y, n_chip // n_y)
    in_specs = (
        P("seq", "tp"),
        P("seq", "tp"),
        P(),
        P(None, "tp"),
        P(None, "tp"),
        P(None, "tp"),
        P("tp", None),
    )
    return jax.shard_map(
        functools.partial(on_device, sizes),
        mesh=mesh,
        in_specs=in_specs,
        out_specs=(P("seq", "tp"), P("seq", "tp")),
        check_vma=False,
    )
```

time: 521 us -> 132 us (0.25)
  starting transfers between devices: 291 us -> 0 us
  Pallas kernels: 0 us -> 123 us
  blocking collectives: 117 us -> 0 us
  waiting for transfers between devices: 35.3 us -> 0 us
  matrix products: 21.5 us -> 0 us
  between operations: 17.9 us -> 0.66 us
  local copies, waits for them, and re-layouts: 21.6 us -> 7.9 us
  other arithmetic: 13.2 us -> 0 us
    ppermute x80 -> x0, starting transfers between devices: 274 us -> none  [shifted(): return lax.ppermute(array, axis, pairs)]
    pallas_call x0 -> x1, Pallas kernels: none -> 123 us  [on_device(): pl.pallas_call(functools.partial(kernel, sizes), out_shape=(shape, shape)...]
    psum x4 -> x0, blocking collectives: 70.5 us -> none  [over_axes(): array = lax.psum(array, axis)]
    all_to_all x5 -> x0, blocking collectives: 46.1 us -> none  [the longest x3 23.7 us: from_everyone(): return lax.all_to_all(copies, axis, split_axis=0, concat_axis=0, tiled=True)]
    dot_general x29 -> x0, matrix products: 21.5 us -> none  [the longest x4 5.97 us: on_device(): jnp.einsum('rhe,khe->hrk', grad_out, values_all, preferred_element_type=j...]
    ppermute x80 -> x0, waiting for transfers between devices: 17.8 us -> none  [shifted(): return lax.ppermute(array, axis, pairs)]
    all_to_all x4 -> x0, waiting for transfers between devices: 17.5 us -> none  [the longest x2 13.6 us: summed_on_arrival(): lax.all_to_all(parts, axis, split_axis=0, concat_axis=0, tiled=True)]
    all_to_all x4 -> x0, starting transfers between devices: 16.3 us -> none  [the longest x2 8.25 us: from_everyone(): return lax.all_to_all(copies, axis, split_axis=0, concat_axis=0, tiled=True)]
  transfers between devices with their start and end apart: 84 -> 0, of which waited for: 10 -> 0; matrix products, arithmetic and copies ran while one was open for 2% -> 0% of each run, Pallas kernels for 0% -> 0%
where the time goes in v1:
time: 132 us
  Pallas kernels  123 us (93%)
  local copies, waits for them, and re-layouts  7.9 us (6%)
    pallas_call x1, Pallas kernels, on_device(): pl.pallas_call(functools.partial(kernel, sizes), out_shape=(shape, shape)...  123 us
    unnamed x16, local copies, waits for them, and re-layouts  7.9 us

profile of v1, /device:TPU:1, one launch (start us, length us, event | category | flops | bytes accessed | tf_op | source)
XLA Modules:
  0.0 131.8 jit_solution(9310722810188272229)
XLA Ops:
  0.6 0.0 copy-start
  0.6 1.0 copy-done
  1.7 0.0 copy-start.1
  1.7 1.0 copy-done.1
  2.7 0.0 copy-start.2
  2.7 1.0 copy-done.2
  3.8 0.0 copy-start.3
  3.8 1.0 copy-done.3
  4.8 0.0 copy-start.4
  4.8 0.9 copy-done.4
  5.7 0.0 copy-start.5
  5.7 0.8 copy-done.5
  6.5 0.0 copy-start.6
  6.5 0.7 copy-done.6
  7.2 123.2 %block.1 = (f32[128,256]{1,0:T(8,128)S(1)}, f32[128,256]{1,0:T(8,128)S(1)}) custom-call(bf16[128,256]{1,0:T(8,128)(2,1)S(1)} %copy-done.5, f32[128,256]{1,0:T(8,128)S(1)} %copy-done.4, f32[1,1024]{1,0:T(1,128)S(1)} %bitcast.1, bf16[1024,256]{1,0:T(8,128)(2,1)S(1)} %copy-done, bf16[1024,256]{1,0:T(8,128)(2,1)S(1)} %copy-done.1, ...), custom_call_target="tpu_custom_call" | custom-call | tf_op jit(solution)/shard_map/block/pallas_call | solution.py:569
  130.5 0.7 copy.11
  131.1 0.7 copy.12
Async XLA Ops:
  0.6 1.0 copy-start
  1.7 1.0 copy-start.1
  2.7 1.0 copy-start.2
  3.8 1.0 copy-start.3
  4.8 0.9 copy-start.4
  5.7 0.8 copy-start.5
  6.5 0.7 copy-start.6

commit v2 on v1

v2 whole, which is shorter than its diff:
```python
import functools
import math

import jax
import jax.numpy as jnp
from jax import lax
from jax.experimental import pallas as pl
from jax.experimental.pallas import tpu as pltpu
from jax.sharding import PartitionSpec as P

HD = 128
HALF = 512
SSTEP = 4
EPSILON = 1e-05
TOK = 128
CHIP = 2 * TOK
SPAN = CHIP + 2 * HALF
REACH = HALF // CHIP
CHUNKS = 2 * REACH + 1
BLOCKS = 4
BT = TOK // BLOCKS
SCALE = 1.0 / math.sqrt(HD)
LOW = -1e30
MESH = pl.DeviceIdType.MESH
F32 = jnp.float32
BF16 = jnp.bfloat16

NT = (((1,), (1,)), ((), ()))
NN = (((1,), (0,)), ((), ()))


def dot(a, b, dims):
    return lax.dot_general(a, b, dims, preferred_element_type=F32)


def wait_for(ref, sem):
    pltpu.make_async_copy(ref, ref, sem).wait()


def kernel(
    sizes,
    state,
    cot,
    gain,
    w_query,
    w_key,
    w_value,
    w_out,
    adj_out,
    res_out,
    w_in,
    w_o,
    gain_v,
    xs,
    xg,
    qkv,
    win,
    att_head,
    att_own,
    stats,
    probs,
    probs_t,
    probs_tb,
    g_msg,
    g_win,
    c_msg,
    c_win,
    g_full,
    g_swap,
    rs_acc,
    rs_send,
    rs_recv,
    kry,
    dif,
    inv_v,
    tile,
    rows_out,
    rows_in,
    outs,
    sem_load,
    sem_xs_s,
    sem_xs_r,
    sem_xg_s,
    sem_xg_r,
    sem_q_s,
    sem_q_r,
    sem_a_s,
    sem_a_r,
    sem_st_s,
    sem_st_r,
    sem_g_s,
    sem_g_r,
    sem_c_s,
    sem_c_r,
    sem_sw_s,
    sem_sw_r,
    sem_rs_s,
    sem_rs_r,
    sem_t_s,
    sem_t_r,
    sem_out,
):
    n_seq, n_tp, n_y, n_z = sizes
    n_chip = n_seq // 2
    s = lax.axis_index("seq")
    tp = lax.axis_index("tp")
    chip = lax.div(s, 2)
    core = lax.rem(s, 2)
    y = lax.rem(chip, n_y)
    z = lax.div(chip, n_y)
    other = 1 - core
    cols = xs.shape[2]
    pair = (2 * chip + other, tp)

    def at_tp(offset):
        return lax.rem(tp + offset, n_tp)

    def at_chip(offset):
        return lax.rem(chip + offset + n_chip, n_chip)

    tp_far = sorted(range(1, n_tp), key=lambda o: -min(o, n_tp - o))
    halo = [d for k in range(REACH, 0, -1) for d in (-k, k)]
    blocks = [slice(b * BT, (b + 1) * BT) for b in range(BLOCKS)]
    stage_a = [
        (2 * (z * n_y + lax.rem(y + oy, n_y)) + lax.rem(core + oc, 2), tp)
        for oy in range(n_y)
        for oc in range(2)
        if (oy, oc) != (0, 0)
    ]
    stage_b = [
        (2 * (lax.rem(z + oz, n_z) * n_y + y) + core, at_tp(ox))
        for oz in range(n_z)
        for ox in range(n_tp)
        if (oz, ox) != (0, 0)
    ]

    def send(src, dst, ssem, rsem, device):
        pltpu.make_async_remote_copy(
            src_ref=src,
            dst_ref=dst,
            send_sem=ssem,
            recv_sem=rsem,
            device_id=device,
            device_id_type=MESH,
        ).start()

    loads = [
        (state, xs.at[tp]),
        (cot, kry.at[0]),
        (gain, gain_v),
        (w_query, w_in.at[0]),
        (w_key, w_in.at[1]),
        (w_value, w_in.at[2]),
        (w_out, w_o),
    ]
    loading = [
        pltpu.make_async_copy(src, dst, sem_load.at[k])
        for k, (src, dst) in enumerate(loads)
    ]
    for copy in loading:
        copy.start()

    barrier = pltpu.get_barrier_semaphore()
    greeted = stage_a + stage_b
    for d in halo:
        for h in range(2):
            greeted.append((2 * at_chip(d) + h, tp))
    for device in greeted:
        pl.semaphore_signal(barrier, inc=1, device_id=device, device_id_type=MESH)
    pl.semaphore_wait(barrier, len(greeted))

    for b in range(BLOCKS):
        for o in tp_far:
            send(
                state.at[pl.ds(b * BT, BT)],
                xs.at[tp, pl.ds(b * BT, BT)],
                sem_xs_s,
                sem_xs_r.at[b],
                (s, at_tp(o)),
            )

    def send_vector(n, b):
        for o in tp_far:
            send(
                xg.at[n, tp, pl.ds(b * BT, BT)],
                xg.at[n, tp, pl.ds(b * BT, BT)],
                sem_xg_s.at[n],
                sem_xg_r.at[n, b],
                (s, at_tp(o)),
            )

    def slot_rows(d, b):
        start = (2 * (REACH - d) + core) * TOK + b * BT
        return pl.ds(pl.multiple_of(start, BT), BT)

    def send_window(t, b):
        rows = pl.ds(b * BT, BT)
        send(
            qkv.at[t, other, rows],
            win.at[t, slot_rows(0, b)],
            sem_q_s,
            sem_q_r.at[t, REACH],
            pair,
        )
        for d in halo:
            for h in range(2):
                send(
                    qkv.at[t, h, rows],
                    win.at[t, slot_rows(d, b)],
                    sem_q_s,
                    sem_q_r.at[t, REACH - d],
                    (2 * at_chip(d) + h, tp),
                )
        win[t, slot_rows(0, b), :] = qkv[t, core, b * BT : (b + 1) * BT, :]

    loading[0].wait()
    loading[2].wait()
    for b, rows in enumerate(blocks):
        wait_for(xs.at[pl.ds(0, n_tp - 1), pl.ds(0, BT)], sem_xs_r.at[b])
        if b == BLOCKS - 1:
            loading[1].wait()
            xg[0, tp] = kry[0].astype(BF16)
            for c in range(BLOCKS):
                send_vector(0, c)
        total = jnp.zeros((BT, 1), F32)
        for r in range(n_tp):
            block = xs[r, rows, :].astype(F32)
            total = total + jnp.sum(block * block, axis=1, keepdims=True)
        inverse = lax.rsqrt(total * (1.0 / (n_tp * cols)) + EPSILON)
        inv_v[rows, :] = jnp.broadcast_to(inverse, (BT, HD))
        normed = jnp.concatenate(
            [
                (
                    xs[r, rows, :].astype(F32)
                    * inverse
                    * gain_v[:, r * cols : (r + 1) * cols]
                ).astype(BF16)
                for r in range(n_tp)
            ],
            axis=1,
        )
        for t in (1, 2, 0):
            if b == 0:
                loading[3 + t].wait()
            acc = dot(normed, w_in[t], NN).astype(BF16)
            for h in range(2):
                qkv[t, h, rows, :] = acc[:, h * HD : (h + 1) * HD]
            if t != 0:
                send_window(t, b)
    for b in range(BLOCKS):
        send_window(0, b)

    def wait_window(t, k):
        rows = TOK if k == REACH else CHIP
        wait_for(win.at[t, pl.ds(0, rows)], sem_q_r.at[t, k])

    def send_grad_out(n, b, rows):
        wait_for(xg.at[n, pl.ds(0, n_tp - 1), pl.ds(0, BT)], sem_xg_r.at[n, b])
        acc = jnp.zeros((BT, 2 * HD), F32)
        for r in range(n_tp):
            acc = acc + dot(xg[n, r, rows, :], w_o[:, r * cols : (r + 1) * cols], NT)
        acc = acc.astype(BF16)
        for h in range(2):
            g_msg[n, h, rows, :] = acc[:, h * HD : (h + 1) * HD]
        taken = pl.ds(b * BT, BT)
        send(
            g_msg.at[n, other, taken],
            g_win.at[n, slot_rows(0, b)],
            sem_g_s.at[n],
            sem_g_r.at[n, REACH],
            pair,
        )
        for d in halo:
            for h in range(2):
                send(
                    g_msg.at[n, h, taken],
                    g_win.at[n, slot_rows(d, b)],
                    sem_g_s.at[n],
                    sem_g_r.at[n, REACH - d],
                    (2 * at_chip(d) + h, tp),
                )
        g_win[n, slot_rows(0, b), :] = g_msg[n, core, rows, :]

    def send_corr(n):
        for h in range(2):
            c_msg[n, h] = jnp.sum(
                (g_msg[n, h].astype(F32) * att_own[h]).T, axis=0, keepdims=True
            )
        send(
            c_msg.at[n, other],
            c_win.at[n, 2 * REACH + core],
            sem_c_s.at[n],
            sem_c_r.at[n, REACH],
            pair,
        )
        for d in halo:
            for h in range(2):
                send(
                    c_msg.at[n, h],
                    c_win.at[n, 2 * (REACH - d) + core],
                    sem_c_s.at[n],
                    sem_c_r.at[n, REACH - d],
                    (2 * at_chip(d) + h, tp),
                )
        c_win[n, 2 * REACH + core] = c_msg[n, core]

    loading[6].wait()
    for b, rows in enumerate(blocks):
        send_grad_out(0, b, rows)

    arrival = sorted(range(CHUNKS), key=lambda k: abs(k - REACH))
    own = slice(HALF, HALF + CHIP)

    def valid(k):
        row = lax.broadcasted_iota(jnp.int32, (CHIP, CHIP), 0)
        col = lax.broadcasted_iota(jnp.int32, (CHIP, CHIP), 1) + k * CHIP
        place = chip * CHIP - HALF + col
        away = row + HALF - col
        return (
            (away <= HALF)
            & (away >= -HALF)
            & (place >= 0)
            & (place < n_chip * CHIP)
        )

    def part(k):
        return slice(k * CHIP, (k + 1) * CHIP)

    wait_window(0, REACH)
    queries = win[0, own, :]
    peak = jnp.full((CHIP, 1), LOW, F32)
    for k in arrival:
        wait_window(1, k)
        scores = dot(queries, win[1, part(k), :], NT) * SCALE
        scores = jnp.where(valid(k), scores, LOW)
        probs[:, part(k)] = scores
        peak = jnp.maximum(peak, jnp.max(scores, axis=1, keepdims=True))
    mass = jnp.zeros((CHIP, 1), F32)
    for k in arrival:
        raw = jnp.exp(probs[:, part(k)] - peak)
        probs[:, part(k)] = raw
        mass = mass + jnp.sum(raw, axis=1, keepdims=True)
    share = 1.0 / mass
    both = jnp.concatenate(
        [
            jnp.broadcast_to(peak, (CHIP, HD)).T[0:1],
            jnp.broadcast_to(share, (CHIP, HD)).T[0:1],
            jnp.zeros((6, CHIP), F32),
        ],
        axis=0,
    )
    stats[REACH] = both
    for d in halo:
        send(
            stats.at[REACH],
            stats.at[REACH - d],
            sem_st_s,
            sem_st_r,
            (2 * at_chip(d) + core, tp),
        )
    attended = jnp.zeros((CHIP, HD), F32)
    for k in arrival:
        wait_window(2, k)
        weights = probs[:, part(k)] * share
        probs[:, part(k)] = weights * SCALE
        attended = attended + dot(weights.astype(BF16), win[2, part(k), :], NN)
    att_head[...] = attended
    other_half = pl.ds(pl.multiple_of(other * TOK, TOK), TOK)
    own_half = pl.ds(pl.multiple_of(core * TOK, TOK), TOK)
    send(att_head.at[other_half], att_own.at[core], sem_a_s, sem_a_r, pair)
    att_own[core] = att_head[own_half, :]
    wait_for(att_own.at[0], sem_a_r)
    send_corr(0)

    keys = win[1, own, :]
    values = win[2, own, :]
    wait_for(stats.at[pl.ds(0, CHUNKS - 1)], sem_st_r)
    for k in arrival:
        if k != REACH:
            wait_window(0, k)
        scores = dot(keys, win[0, part(k), :], NT) * SCALE
        pair_stats = stats[k]
        scores = jnp.where(valid(k), scores - pair_stats[0:1], LOW)
        weights = jnp.exp(scores) * pair_stats[1:2]
        probs_t[:, part(k)] = weights * SCALE
        probs_tb[:, part(k)] = weights.astype(BF16)

    gain_own = gain_v[:, pl.ds(pl.multiple_of(tp * cols, cols), cols)]

    def inner_row(a, b):
        row = jnp.sum(dif[a] * (kry[0] if b is None else dif[b]), axis=0, keepdims=True)
        folded = row[:, 0:HD]
        for start in range(HD, cols, HD):
            folded = folded + row[:, start : start + HD]
        return folded

    pairs = [(a, b) for a in range(SSTEP) for b in list(range(a + 1)) + [None]]

    def inner_rows(a):
        for place, (first, second) in enumerate(pairs):
            if first == a:
                tile[place : place + 1, :] = inner_row(first, second)

    tile[...] = jnp.zeros(tile.shape, F32)

    def product(n, carry):
        def give_back(t, whole):
            whole = whole.astype(BF16)
            first, second = whole[0:TOK], whole[TOK:CHIP]
            mine = core == 0
            g_full[n, core, t] = jnp.where(mine, first, second)
            g_swap[n, t] = jnp.where(mine, second, first)

        def both_heads(t):
            return jnp.concatenate([g_full[n, 0, t], g_full[n, 1, t]], axis=1)

        def tp_rows(o):
            return pl.ds(pl.multiple_of(at_tp(o) * cols, cols), cols)

        wait_for(g_win.at[n, pl.ds(0, TOK)], sem_g_r.at[n, REACH])
        grad = g_win[n, own, :]
        corr = jnp.sum(grad.astype(F32) * att_head[...], axis=1, keepdims=True)
        grad_q = jnp.zeros((CHIP, HD), F32)
        for k in range(CHUNKS):
            grad_p = dot(grad, win[2, part(k), :], NT)
            score = (probs[:, part(k)] * (grad_p - corr)).astype(BF16)
            grad_q = grad_q + dot(score, win[1, part(k), :], NN)
        give_back(0, grad_q)
        send(
            g_swap.at[n, pl.ds(0, 1)],
            g_full.at[n, core, pl.ds(0, 1)],
            sem_sw_s.at[n],
            sem_sw_r.at[n, 0],
            pair,
        )
        grad_k = jnp.zeros((CHIP, HD), F32)
        grad_v = jnp.zeros((CHIP, HD), F32)
        for k in arrival:
            if k != REACH:
                wait_for(g_win.at[n, pl.ds(0, CHIP)], sem_g_r.at[n, k])
            wait_for(c_win.at[n, pl.ds(0, 1 if k == REACH else 2)], sem_c_r.at[n, k])
            grad = g_win[n, part(k), :]
            corr = jnp.concatenate([c_win[n, 2 * k], c_win[n, 2 * k + 1]], axis=1)
            grad_p = dot(values, grad, NT)
            score = (probs_t[:, part(k)] * (grad_p - corr)).astype(BF16)
            grad_k = grad_k + dot(score, win[0, part(k), :], NN)
            grad_v = grad_v + dot(probs_tb[:, part(k)], grad, NN)
            if k == REACH:
                wait_for(g_swap.at[n, pl.ds(0, 1)], sem_sw_r.at[n, 0])
                for o in range(n_tp):
                    rs_acc[o] = dot(both_heads(0), w_in[0, tp_rows(o), :], NT)
        give_back(1, grad_k)
        give_back(2, grad_v)
        send(
            g_swap.at[n, pl.ds(1, 2)],
            g_full.at[n, core, pl.ds(1, 2)],
            sem_sw_s.at[n],
            sem_sw_r.at[n, 1],
            pair,
        )
        wait_for(g_swap.at[n, pl.ds(1, 2)], sem_sw_r.at[n, 1])
        late = [both_heads(1), both_heads(2)]

        def partial_sum(o):
            acc = rs_acc[o]
            for t in range(2):
                acc = acc + dot(late[t], w_in[1 + t, tp_rows(o), :], NT)
            return acc

        def send_sum(o, b):
            send(
                rs_send.at[n, o - 1, pl.ds(b * BT, BT)],
                rs_recv.at[n, o - 1, pl.ds(b * BT, BT)],
                sem_rs_s.at[n],
                sem_rs_r.at[n, b],
                (s, at_tp(o)),
            )

        for o in tp_far:
            rs_send[n, o - 1] = partial_sum(o).astype(BF16)
            send_sum(o, 0)
        for b in range(1, BLOCKS):
            for o in tp_far:
                send_sum(o, b)
        rs_acc[0] = partial_sum(0)
        for b, rows in enumerate(blocks):
            wait_for(
                rs_recv.at[n, pl.ds(0, n_tp - 1), pl.ds(0, BT)], sem_rs_r.at[n, b]
            )
            summed = rs_acc[0, rows, :]
            for o in range(1, n_tp):
                summed = summed + rs_recv[n, o - 1, rows, :].astype(F32)
            inverse = jnp.concatenate([inv_v[rows, :]] * (cols // HD), axis=1)
            vector = inverse * (gain_own * summed)

            @pl.when(n < SSTEP - 1)
            def _():
                xg[n + 1, tp, rows, :] = vector.astype(BF16)
                send_vector(n + 1, b)

            kry[n + 1, rows, :] = vector
            dif[n, rows, :] = kry[n, rows, :] - vector

        @pl.when(n < SSTEP - 1)
        def _():
            for b, rows in enumerate(blocks):
                send_grad_out(n + 1, b, rows)
            send_corr(n + 1)

        for a in range(SSTEP):

            @pl.when(n == a)
            def _():
                inner_rows(a)

        return carry

    lax.fori_loop(0, SSTEP, product, 0)

    square = jnp.concatenate(
        [tile[...], jnp.zeros((HD - tile.shape[0], HD), F32)], axis=0
    )
    whole = jnp.sum(square.T, axis=0, keepdims=True)
    start = 0
    for stage, devices in enumerate((stage_a, stage_b)):
        rows_out[stage] = whole
        for k, device in enumerate(devices):
            send(
                rows_out.at[stage],
                rows_in.at[start + k],
                sem_t_s,
                sem_t_r.at[stage],
                device,
            )
        wait_for(rows_in.at[pl.ds(start, len(devices))], sem_t_r.at[stage])
        whole = whole + jnp.sum(rows_in[start : start + len(devices)], axis=0)
        start += len(devices)
    spread = jnp.broadcast_to(whole, (HD, HD)).T

    def inner(a, b):
        place = pairs.index((a, b))
        return spread[place : place + 1]

    factor = {}
    for a in range(SSTEP):
        for b in range(a + 1):
            value = inner(a, b)
            for c in range(b):
                value = value - factor[a, c] * factor[b, c]
            factor[a, b] = jnp.sqrt(value) if a == b else value / factor[b, b]
    half = []
    for a in range(SSTEP):
        value = inner(a, None)
        for b in range(a):
            value = value - factor[a, b] * half[b]
        half.append(value / factor[a, a])
    coef = [None] * SSTEP
    for a in range(SSTEP - 1, -1, -1):
        value = half[a]
        for b in range(a + 1, SSTEP):
            value = value - factor[b, a] * coef[b]
        coef[a] = value / factor[a, a]
    coef = [jnp.concatenate([c] * (cols // HD), axis=1) for c in coef]
    adjoint = coef[0] * kry[0]
    for n in range(1, SSTEP):
        adjoint = adjoint + coef[n] * kry[n]
    outs[0] = adjoint
    out_a = pltpu.make_async_copy(outs.at[0], adj_out, sem_out.at[0])
    out_a.start()
    residual = kry[0]
    for n in range(SSTEP):
        residual = residual - coef[n] * dif[n]
    outs[1] = residual
    out_b = pltpu.make_async_copy(outs.at[1], res_out, sem_out.at[1])
    out_b.start()

    sent = 4 * REACH + 1
    wait_for(xs.at[pl.ds(0, n_tp - 1)], sem_xs_s)
    wait_for(win.at[:, pl.ds(0, sent * TOK)], sem_q_s)
    wait_for(att_own.at[0], sem_a_s)
    wait_for(stats.at[pl.ds(0, CHUNKS - 1)], sem_st_s)
    for n in range(SSTEP):
        wait_for(xg.at[n, pl.ds(0, n_tp - 1)], sem_xg_s.at[n])
        wait_for(g_win.at[n, pl.ds(0, sent * TOK)], sem_g_s.at[n])
        wait_for(c_win.at[n, pl.ds(0, sent)], sem_c_s.at[n])
        wait_for(g_swap.at[n], sem_sw_s.at[n])
        wait_for(rs_send.at[n], sem_rs_s.at[n])
    wait_for(rows_in, sem_t_s)
    out_a.wait()
    out_b.wait()


def on_device(sizes, state, cotangent, norm_gain, w_query, w_key, w_value, w_out):
    n_seq, n_tp, n_y, n_z = sizes
    tok, cols = state.shape
    width = n_tp * cols
    row_count = (2 * n_y - 1) + (n_z * n_tp - 1)
    dma = pltpu.SemaphoreType.DMA
    scratch = [
        pltpu.VMEM((3, width, 2 * HD), BF16),
        pltpu.VMEM((2 * HD, width), BF16),
        pltpu.VMEM((1, width), F32),
        pltpu.VMEM((n_tp, tok, cols), BF16),
        pltpu.VMEM((SSTEP, n_tp, tok, cols), BF16),
        pltpu.VMEM((3, 2, tok, HD), BF16),
        pltpu.VMEM((3, SPAN, HD), BF16),
        pltpu.VMEM((CHIP, HD), F32),
        pltpu.VMEM((2, tok, HD), F32),
        pltpu.VMEM((CHUNKS, 8, CHIP), F32),
        pltpu.VMEM((CHIP, SPAN), F32),
        pltpu.VMEM((CHIP, SPAN), F32),
        pltpu.VMEM((CHIP, SPAN), BF16),
        pltpu.VMEM((SSTEP, 2, tok, HD), BF16),
        pltpu.VMEM((SSTEP, SPAN, HD), BF16),
        pltpu.VMEM((SSTEP, 2, 1, HD), F32),
        pltpu.VMEM((SSTEP, 2 * CHUNKS, 1, HD), F32),
        pltpu.VMEM((SSTEP, 2, 3, tok, HD), BF16),
        pltpu.VMEM((SSTEP, 3, tok, HD), BF16),
        pltpu.VMEM((n_tp, tok, cols), F32),
        pltpu.VMEM((SSTEP, n_tp - 1, tok, cols), BF16),
        pltpu.VMEM((SSTEP, n_tp - 1, tok, cols), BF16),
        pltpu.VMEM((SSTEP + 1, tok, cols), F32),
        pltpu.VMEM((SSTEP, tok, cols), F32),
        pltpu.VMEM((tok, HD), F32),
        pltpu.VMEM((16, HD), F32),
        pltpu.VMEM((2, 1, HD), F32),
        pltpu.VMEM((row_count, 1, HD), F32),
        pltpu.VMEM((2, tok, cols), F32),
        dma((7,)),
        dma,
        dma((BLOCKS,)),
        dma((SSTEP,)),
        dma((SSTEP, BLOCKS)),
        dma,
        dma((3, CHUNKS)),
        dma,
        dma,
        dma,
        dma,
        dma((SSTEP,)),
        dma((SSTEP, CHUNKS)),
        dma((SSTEP,)),
        dma((SSTEP, CHUNKS)),
        dma((SSTEP,)),
        dma((SSTEP, 2)),
        dma((SSTEP,)),
        dma((SSTEP, BLOCKS)),
        dma,
        dma((2,)),
        dma((2,)),
    ]
    anywhere = pl.BlockSpec(memory_space=pl.ANY)
    shape = jax.ShapeDtypeStruct((tok, cols), F32)
    return pl.pallas_call(
        functools.partial(kernel, sizes),
        out_shape=(shape, shape),
        in_specs=[anywhere] * 7,
        out_specs=(anywhere, anywhere),
        scratch_shapes=scratch,
        compiler_params=pltpu.CompilerParams(
            collective_id=0, has_side_effects=True, vmem_limit_bytes=63 * 2**20
        ),
        name="block",
    )(state, cotangent, norm_gain.reshape(1, width), w_query, w_key, w_value, w_out)


def solution(mesh):
    n_seq, n_tp = mesh.shape["seq"], mesh.shape["tp"]
    n_chip = n_seq // 2
    n_y = 1
    while n_y * n_y < n_chip:
        n_y *= 2
    sizes = (n_seq, n_tp, n_y, n_chip // n_y)
    in_specs = (
        P("seq", "tp"),
        P("seq", "tp"),
        P(),
        P(None, "tp"),
        P(None, "tp"),
        P(None, "tp"),
        P("tp", None),
    )
    return jax.shard_map(
        functools.partial(on_device, sizes),
        mesh=mesh,
        in_specs=in_specs,
        out_specs=(P("seq", "tp"), P("seq", "tp")),
        check_vma=False,
    )
```

time: 132 us -> 117 us (0.89)
  Pallas kernels: 123 us -> 114 us
  local copies, waits for them, and re-layouts: 7.9 us -> 2.26 us
    pallas_call x1, Pallas kernels: 123 us -> 114 us  [on_device(): pl.pallas_call(functools.partial(kernel, sizes), out_shape=(shape, shape)...]
    unnamed x16 -> x4, local copies, waits for them, and re-layouts: 7.9 us -> 2.26 us
where the time goes in v2:
time: 117 us
  Pallas kernels  114 us (97%)
  local copies, waits for them, and re-layouts  2.26 us (2%)
    pallas_call x1, Pallas kernels, on_device(): pl.pallas_call(functools.partial(kernel, sizes), out_shape=(shape, shape)...  114 us

profile of v2, /device:TPU:1, one launch (start us, length us, event | category | flops | bytes accessed | tf_op | source)
XLA Modules:
  0.0 117.1 jit_solution(8094110751229100615)
XLA Ops:
  0.6 114.2 %block.1 = (f32[128,256]{1,0:T(8,128)}, f32[128,256]{1,0:T(8,128)}) custom-call(bf16[128,256]{1,0:T(8,128)(2,1)} %state.1, f32[128,256]{1,0:T(8,128)} %cot.1, f32[1,1024]{1,0:T(1,128)} %bitcast.1, bf16[1024,256]{1,0:T(8,128)(2,1)} %w_query.1, bf16[1024,256]{1,0:T(8,128)(2,1)} %w_key.1, bf16[1024,256]{1,0:T(8,128)(2,1)} %w_value.1, bf16[256,1024]{1,0:T(8,128)(2,1)} %w_out.1), custom_call_target="tpu_custom_call" | custom-call | tf_op jit(solution)/shard_map/block/pallas_call | solution.py:654
  114.8 0.0 copy-start
  114.8 1.6 %copy.11 = f32[128,256]{1,0:T(8,128)} copy(f32[128,256]{1,0:T(8,128)} %get-tuple-element.4) | data formatting | bytes 262144
  116.4 0.0 copy-done
  116.4 0.7 copy.12
Async XLA Ops:
  114.8 1.6 %copy-start = (f32[128,256]{1,0:T(8,128)S(1)}, f32[128,256]{1,0:T(8,128)}, u32[]{:S(2)}) copy-start(f32[128,256]{1,0:T(8,128)} %get-tuple-element.5) | copy-start | bytes 393220

commit v3 on v2

--- a/solution.py
+++ b/solution.py
@@ -48,10 +48,12 @@
     w_out,
     adj_out,
     res_out,
-    w_in,
+    w_q,
+    w_kv,
     w_o,
     gain_v,
     xs,
+    normed_v,
     xg,
     qkv,
     win,
@@ -67,6 +69,7 @@
     c_win,
     g_full,
     g_swap,
+    kv_acc,
     rs_acc,
     rs_send,
     rs_recv,
@@ -76,13 +79,13 @@
     tile,
     rows_out,
     rows_in,
-    outs,
     sem_load,
     sem_xs_s,
     sem_xs_r,
     sem_xg_s,
     sem_xg_r,
     sem_q_s,
+    sem_kv_r,
     sem_q_r,
     sem_a_s,
     sem_a_r,
@@ -98,7 +101,6 @@
     sem_rs_r,
     sem_t_s,
     sem_t_r,
-    sem_out,
 ):
     n_seq, n_tp, n_y, n_z = sizes
     n_chip = n_seq // 2
@@ -119,6 +121,7 @@
         return lax.rem(chip + offset + n_chip, n_chip)
 
     tp_far = sorted(range(1, n_tp), key=lambda o: -min(o, n_tp - o))
+    near = (-1, 1)
     halo = [d for k in range(REACH, 0, -1) for d in (-k, k)]
     blocks = [slice(b * BT, (b + 1) * BT) for b in range(BLOCKS)]
     stage_a = [
@@ -144,22 +147,6 @@
             device_id_type=MESH,
         ).start()
 
-    loads = [
-        (state, xs.at[tp]),
-        (cot, kry.at[0]),
-        (gain, gain_v),
-        (w_query, w_in.at[0]),
-        (w_key, w_in.at[1]),
-        (w_value, w_in.at[2]),
-        (w_out, w_o),
-    ]
-    loading = [
-        pltpu.make_async_copy(src, dst, sem_load.at[k])
-        for k, (src, dst) in enumerate(loads)
-    ]
-    for copy in loading:
-        copy.start()
-
     barrier = pltpu.get_barrier_semaphore()
     greeted = stage_a + stage_b
     for d in halo:
@@ -167,6 +154,27 @@
             greeted.append((2 * at_chip(d) + h, tp))
     for device in greeted:
         pl.semaphore_signal(barrier, inc=1, device_id=device, device_id_type=MESH)
+
+    loads = [
+        (cot, kry.at[0]),
+        (state, xs.at[tp]),
+        (gain, gain_v),
+    ]
+    for h in range(2):
+        for t, source in enumerate((w_key, w_value)):
+            loads.append(
+                (
+                    source.at[:, pl.ds(h * HD, HD)],
+                    w_kv.at[h, :, pl.ds(t * HD, HD)],
+                )
+            )
+    loads += [(w_query, w_q), (w_out, w_o)]
+    loading = [
+        pltpu.make_async_copy(src, dst, sem_load.at[k])
+        for k, (src, dst) in enumerate(loads)
+    ]
+    for copy in loading:
+        copy.start()
     pl.semaphore_wait(barrier, len(greeted))
 
     for b in range(BLOCKS):
@@ -193,32 +201,57 @@
         start = (2 * (REACH - d) + core) * TOK + b * BT
         return pl.ds(pl.multiple_of(start, BT), BT)
 
-    def send_window(t, b):
-        rows = pl.ds(b * BT, BT)
-        send(
-            qkv.at[t, other, rows],
-            win.at[t, slot_rows(0, b)],
-            sem_q_s,
-            sem_q_r.at[t, REACH],
-            pair,
-        )
-        for d in halo:
+    def send_window(t, count, start, size, rsem):
+        rows = pl.ds(start, size)
+        place = pl.ds(t, count)
+
+        def target(d):
+            first = (2 * (REACH - d) + core) * TOK + start
+            return win.at[place, pl.ds(pl.multiple_of(first, BT), size)]
+
+        send(qkv.at[other, place, rows], target(0), sem_q_s, rsem(REACH), pair)
+        for d in near:
             for h in range(2):
                 send(
-                    qkv.at[t, h, rows],
-                    win.at[t, slot_rows(d, b)],
+                    qkv.at[h, place, rows],
+                    target(d),
                     sem_q_s,
-                    sem_q_r.at[t, REACH - d],
+                    rsem(REACH - d),
                     (2 * at_chip(d) + h, tp),
                 )
-        win[t, slot_rows(0, b), :] = qkv[t, core, b * BT : (b + 1) * BT, :]
-
-    loading[0].wait()
+        own_rows = pl.ds(
+            pl.multiple_of((2 * REACH + core) * TOK + start, BT), size
+        )
+        for k in range(t, t + count):
+            win[k, own_rows, :] = qkv[core, k, start : start + size, :]
+
+    def wait_kv(k, b):
+        rows = BT if k == REACH else 2 * BT
+        wait_for(win.at[pl.ds(1, 2), pl.ds(0, rows)], sem_kv_r.at[k, b])
+
+    def wait_q(k):
+        wait_for(win.at[0, pl.ds(0, TOK if k == REACH else CHIP)], sem_q_r.at[k])
+
+    def pass_on(t, count, starts, size, rsem):
+        for d in near:
+            k = REACH - d
+            for start in starts:
+                first = k * CHIP + start
+                send(
+                    win.at[pl.ds(t, count), pl.ds(first, size)],
+                    win.at[pl.ds(t, count), pl.ds(first - d * CHIP, size)],
+                    sem_q_s,
+                    rsem(k - d),
+                    (2 * at_chip(d) + core, tp),
+                )
+
     loading[2].wait()
     for b, rows in enumerate(blocks):
         wait_for(xs.at[pl.ds(0, n_tp - 1), pl.ds(0, BT)], sem_xs_r.at[b])
+        if b == 0:
+            loading[0].wait()
+            loading[1].wait()
         if b == BLOCKS - 1:
-            loading[1].wait()
             xg[0, tp] = kry[0].astype(BF16)
             for c in range(BLOCKS):
                 send_vector(0, c)
@@ -239,20 +272,24 @@
             ],
             axis=1,
         )
-        for t in (1, 2, 0):
+        normed_v[rows, :] = normed
+        for h in range(2):
             if b == 0:
-                loading[3 + t].wait()
-            acc = dot(normed, w_in[t], NN).astype(BF16)
-            for h in range(2):
-                qkv[t, h, rows, :] = acc[:, h * HD : (h + 1) * HD]
-            if t != 0:
-                send_window(t, b)
+                loading[3 + 2 * h].wait()
+                loading[4 + 2 * h].wait()
+            acc = dot(normed, w_kv[h], NN).astype(BF16)
+            for t in range(2):
+                qkv[h, 1 + t, rows, :] = acc[:, t * HD : (t + 1) * HD]
+        send_window(1, 2, b * BT, BT, lambda k, b=b: sem_kv_r.at[k, b])
+    loading[7].wait()
+    acc = dot(normed_v[...], w_q[...], NN).astype(BF16)
+    for h in range(2):
+        qkv[h, 0] = acc[:, h * HD : (h + 1) * HD]
+    send_window(0, 1, 0, TOK, lambda k: sem_q_r.at[k])
     for b in range(BLOCKS):
-        send_window(0, b)
-
-    def wait_window(t, k):
-        rows = TOK if k == REACH else CHIP
-        wait_for(win.at[t, pl.ds(0, rows)], sem_q_r.at[t, k])
+        for d in near:
+            wait_kv(REACH - d, b)
+        pass_on(1, 2, [b * BT, TOK + b * BT], BT, lambda k, b=b: sem_kv_r.at[k, b])
 
     def send_grad_out(n, b, rows):
         wait_for(xg.at[n, pl.ds(0, n_tp - 1), pl.ds(0, BT)], sem_xg_r.at[n, b])
@@ -304,10 +341,6 @@
                 )
         c_win[n, 2 * REACH + core] = c_msg[n, core]
 
-    loading[6].wait()
-    for b, rows in enumerate(blocks):
-        send_grad_out(0, b, rows)
-
     arrival = sorted(range(CHUNKS), key=lambda k: abs(k - REACH))
     own = slice(HALF, HALF + CHIP)
 
@@ -326,15 +359,28 @@
     def part(k):
         return slice(k * CHIP, (k + 1) * CHIP)
 
-    wait_window(0, REACH)
-    queries = win[0, own, :]
-    peak = jnp.full((CHIP, 1), LOW, F32)
-    for k in arrival:
-        wait_window(1, k)
-        scores = dot(queries, win[1, part(k), :], NT) * SCALE
+    def scores_of(k, peak):
+        scores = dot(win[0, own, :], win[1, part(k), :], NT) * SCALE
         scores = jnp.where(valid(k), scores, LOW)
         probs[:, part(k)] = scores
-        peak = jnp.maximum(peak, jnp.max(scores, axis=1, keepdims=True))
+        return jnp.maximum(peak, jnp.max(scores, axis=1, keepdims=True))
+
+    wait_q(REACH)
+    for b in range(BLOCKS):
+        wait_kv(REACH, b)
+    peak = jnp.full((CHIP, 1), LOW, F32)
+    for k in arrival[:3]:
+        peak = scores_of(k, peak)
+    for d in near:
+        wait_q(REACH - d)
+    pass_on(0, 1, [0], CHIP, lambda k: sem_q_r.at[k])
+    loading[8].wait()
+    for b, rows in enumerate(blocks):
+        send_grad_out(0, b, rows)
+    for k in arrival[3:]:
+        for b in range(BLOCKS):
+            wait_kv(k, b)
+        peak = scores_of(k, peak)
     mass = jnp.zeros((CHIP, 1), F32)
     for k in arrival:
         raw = jnp.exp(probs[:, part(k)] - peak)
@@ -360,7 +406,6 @@
         )
     attended = jnp.zeros((CHIP, HD), F32)
     for k in arrival:
-        wait_window(2, k)
         weights = probs[:, part(k)] * share
         probs[:, part(k)] = weights * SCALE
         attended = attended + dot(weights.astype(BF16), win[2, part(k), :], NN)
@@ -373,11 +418,10 @@
     send_corr(0)
 
     keys = win[1, own, :]
-    values = win[2, own, :]
     wait_for(stats.at[pl.ds(0, CHUNKS - 1)], sem_st_r)
     for k in arrival:
-        if k != REACH:
-            wait_window(0, k)
+        if abs(k - REACH) == 2:
+            wait_q(k)
         scores = dot(keys, win[0, part(k), :], NT) * SCALE
         pair_stats = stats[k]
         scores = jnp.where(valid(k), scores - pair_stats[0:1], LOW)
@@ -433,39 +477,66 @@
             sem_sw_r.at[n, 0],
             pair,
         )
-        grad_k = jnp.zeros((CHIP, HD), F32)
-        grad_v = jnp.zeros((CHIP, HD), F32)
-        for k in arrival:
+        def key_side(k, values, wide, low):
+            grad = g_win[n, part(k), :]
+            corr = jnp.concatenate([c_win[n, 2 * k], c_win[n, 2 * k + 1]], axis=1)
+            score = (wide * (dot(values, grad, NT) - corr)).astype(BF16)
+            return dot(score, win[0, part(k), :], NN), dot(low, grad, NN)
+
+        def wait_grad(k):
             if k != REACH:
                 wait_for(g_win.at[n, pl.ds(0, CHIP)], sem_g_r.at[n, k])
             wait_for(c_win.at[n, pl.ds(0, 1 if k == REACH else 2)], sem_c_r.at[n, k])
-            grad = g_win[n, part(k), :]
-            corr = jnp.concatenate([c_win[n, 2 * k], c_win[n, 2 * k + 1]], axis=1)
-            grad_p = dot(values, grad, NT)
-            score = (probs_t[:, part(k)] * (grad_p - corr)).astype(BF16)
-            grad_k = grad_k + dot(score, win[0, part(k), :], NN)
-            grad_v = grad_v + dot(probs_tb[:, part(k)], grad, NN)
-            if k == REACH:
+
+        for place, k in enumerate(arrival[:3]):
+            wait_grad(k)
+            grad_k, grad_v = key_side(
+                k, win[2, own, :], probs_t[:, part(k)], probs_tb[:, part(k)]
+            )
+            if place == 0:
+                kv_acc[0] = grad_k
+                kv_acc[1] = grad_v
                 wait_for(g_swap.at[n, pl.ds(0, 1)], sem_sw_r.at[n, 0])
                 for o in range(n_tp):
-                    rs_acc[o] = dot(both_heads(0), w_in[0, tp_rows(o), :], NT)
-        give_back(1, grad_k)
-        give_back(2, grad_v)
-        send(
-            g_swap.at[n, pl.ds(1, 2)],
-            g_full.at[n, core, pl.ds(1, 2)],
-            sem_sw_s.at[n],
-            sem_sw_r.at[n, 1],
-            pair,
-        )
+                    rs_acc[o] = dot(both_heads(0), w_q[tp_rows(o), :], NT)
+            else:
+                kv_acc[0] += grad_k
+                kv_acc[1] += grad_v
+        for k in arrival[3:]:
+            wait_grad(k)
+        for token_core in (other, core):
+            taken = pl.ds(pl.multiple_of(token_core * TOK, TOK), TOK)
+            window = pl.ds(pl.multiple_of(HALF + token_core * TOK, TOK), TOK)
+            sums = [kv_acc[0, taken, :], kv_acc[1, taken, :]]
+            for k in arrival[3:]:
+                grad_k, grad_v = key_side(
+                    k,
+                    win[2, window, :],
+                    probs_t[taken, part(k)],
+                    probs_tb[taken, part(k)],
+                )
+                sums = [sums[0] + grad_k, sums[1] + grad_v]
+            for t in range(2):
+                if token_core is other:
+                    g_swap[n, 1 + t] = sums[t].astype(BF16)
+                else:
+                    g_full[n, core, 1 + t] = sums[t].astype(BF16)
+            if token_core is other:
+                send(
+                    g_swap.at[n, pl.ds(1, 2)],
+                    g_full.at[n, core, pl.ds(1, 2)],
+                    sem_sw_s.at[n],
+                    sem_sw_r.at[n, 1],
+                    pair,
+                )
+
+        def partial_sum(o, head):
+            late = jnp.concatenate([g_full[n, head, 1], g_full[n, head, 2]], axis=1)
+            return rs_acc[o] + dot(late, w_kv[head, tp_rows(o), :], NT)
+
+        for o in range(n_tp):
+            rs_acc[o] = partial_sum(o, core)
         wait_for(g_swap.at[n, pl.ds(1, 2)], sem_sw_r.at[n, 1])
-        late = [both_heads(1), both_heads(2)]
-
-        def partial_sum(o):
-            acc = rs_acc[o]
-            for t in range(2):
-                acc = acc + dot(late[t], w_in[1 + t, tp_rows(o), :], NT)
-            return acc
 
         def send_sum(o, b):
             send(
@@ -477,12 +548,12 @@
             )
 
         for o in tp_far:
-            rs_send[n, o - 1] = partial_sum(o).astype(BF16)
+            rs_send[n, o - 1] = partial_sum(o, other).astype(BF16)
             send_sum(o, 0)
         for b in range(1, BLOCKS):
             for o in tp_far:
                 send_sum(o, b)
-        rs_acc[0] = partial_sum(0)
+        rs_acc[0] = partial_sum(0, other)
         for b, rows in enumerate(blocks):
             wait_for(
                 rs_recv.at[n, pl.ds(0, n_tp - 1), pl.ds(0, BT)], sem_rs_r.at[n, b]
@@ -564,15 +635,11 @@
     adjoint = coef[0] * kry[0]
     for n in range(1, SSTEP):
         adjoint = adjoint + coef[n] * kry[n]
-    outs[0] = adjoint
-    out_a = pltpu.make_async_copy(outs.at[0], adj_out, sem_out.at[0])
-    out_a.start()
+    adj_out[...] = adjoint
     residual = kry[0]
     for n in range(SSTEP):
         residual = residual - coef[n] * dif[n]
-    outs[1] = residual
-    out_b = pltpu.make_async_copy(outs.at[1], res_out, sem_out.at[1])
-    out_b.start()
+    res_out[...] = residual
 
     sent = 4 * REACH + 1
     wait_for(xs.at[pl.ds(0, n_tp - 1)], sem_xs_s)
@@ -586,8 +653,6 @@
         wait_for(g_swap.at[n], sem_sw_s.at[n])
         wait_for(rs_send.at[n], sem_rs_s.at[n])
     wait_for(rows_in, sem_t_s)
-    out_a.wait()
-    out_b.wait()
 
 
 def on_device(sizes, state, cotangent, norm_gain, w_query, w_key, w_value, w_out):
@@ -597,12 +662,14 @@
     row_count = (2 * n_y - 1) + (n_z * n_tp - 1)
     dma = pltpu.SemaphoreType.DMA
     scratch = [
-        pltpu.VMEM((3, width, 2 * HD), BF16),
+        pltpu.VMEM((width, 2 * HD), BF16),
+        pltpu.VMEM((2, width, 2 * HD), BF16),
         pltpu.VMEM((2 * HD, width), BF16),
         pltpu.VMEM((1, width), F32),
         pltpu.VMEM((n_tp, tok, cols), BF16),
+        pltpu.VMEM((tok, width), BF16),
         pltpu.VMEM((SSTEP, n_tp, tok, cols), BF16),
-        pltpu.VMEM((3, 2, tok, HD), BF16),
+        pltpu.VMEM((2, 3, tok, HD), BF16),
         pltpu.VMEM((3, SPAN, HD), BF16),
         pltpu.VMEM((CHIP, HD), F32),
         pltpu.VMEM((2, tok, HD), F32),
@@ -616,6 +683,7 @@
         pltpu.VMEM((SSTEP, 2 * CHUNKS, 1, HD), F32),
         pltpu.VMEM((SSTEP, 2, 3, tok, HD), BF16),
         pltpu.VMEM((SSTEP, 3, tok, HD), BF16),
+        pltpu.VMEM((2, CHIP, HD), F32),
         pltpu.VMEM((n_tp, tok, cols), F32),
         pltpu.VMEM((SSTEP, n_tp - 1, tok, cols), BF16),
         pltpu.VMEM((SSTEP, n_tp - 1, tok, cols), BF16),
@@ -625,14 +693,14 @@
         pltpu.VMEM((16, HD), F32),
         pltpu.VMEM((2, 1, HD), F32),
         pltpu.VMEM((row_count, 1, HD), F32),
-        pltpu.VMEM((2, tok, cols), F32),
-        dma((7,)),
+        dma((9,)),
         dma,
         dma((BLOCKS,)),
         dma((SSTEP,)),
         dma((SSTEP, BLOCKS)),
         dma,
-        dma((3, CHUNKS)),
+        dma((CHUNKS, BLOCKS)),
+        dma((CHUNKS,)),
         dma,
         dma,
         dma,
@@ -647,15 +715,13 @@
         dma((SSTEP, BLOCKS)),
         dma,
         dma((2,)),
-        dma((2,)),
     ]
     anywhere = pl.BlockSpec(memory_space=pl.ANY)
-    shape = jax.ShapeDtypeStruct((tok, cols), F32)
     return pl.pallas_call(
         functools.partial(kernel, sizes),
-        out_shape=(shape, shape),
+        out_shape=(pltpu.VMEM((tok, cols), F32), pltpu.VMEM((tok, cols), F32)),
         in_specs=[anywhere] * 7,
-        out_specs=(anywhere, anywhere),
+        out_specs=(pl.BlockSpec(memory_space=pltpu.VMEM),) * 2,
         scratch_shapes=scratch,
         compiler_params=pltpu.CompilerParams(
             collective_id=0, has_side_effects=True, vmem_limit_bytes=63 * 2**20

time: 117 us -> 112 us (0.957)
  Pallas kernels: 114 us -> 110 us
    pallas_call x1, Pallas kernels: 114 us -> 110 us  [on_device(): pl.pallas_call(functools.partial(kernel, sizes), out_shape=(pltpu.VMEM((t...]
where the time goes in v3:
time: 112 us
  Pallas kernels  110 us (98%)
  local copies, waits for them, and re-layouts  1.31 us (1%)
    pallas_call x1, Pallas kernels, on_device(): pl.pallas_call(functools.partial(kernel, sizes), out_shape=(pltpu.VMEM((t...  110 us

profile of v3, /device:TPU:1, one launch (start us, length us, event | category | flops | bytes accessed | tf_op | source)
XLA Modules:
  0.0 112.0 jit_solution(3972930503210555911)
XLA Ops:
  0.6 110.1 %block.1 = (f32[128,256]{1,0:T(8,128)S(1)}, f32[128,256]{1,0:T(8,128)S(1)}) custom-call(bf16[128,256]{1,0:T(8,128)(2,1)} %state.1, f32[128,256]{1,0:T(8,128)} %cot.1, f32[1,1024]{1,0:T(1,128)} %bitcast.1, bf16[1024,256]{1,0:T(8,128)(2,1)} %w_query.1, bf16[1024,256]{1,0:T(8,128)(2,1)} %w_key.1, bf16[1024,256]{1,0:T(8,128)(2,1)} %w_value.1, ...), custom_call_target="tpu_custom_call" | custom-call | tf_op jit(solution)/shard_map/block/pallas_call | solution.py:720
  110.7 0.7 copy.11
  111.4 0.7 copy.12

commit v4 on v3

--- a/solution.py
+++ b/solution.py
@@ -19,6 +19,8 @@
 CHUNKS = 2 * REACH + 1
 BLOCKS = 4
 BT = TOK // BLOCKS
+GRAD_BLOCKS = 4
+GT = TOK // GRAD_BLOCKS
 SCALE = 1.0 / math.sqrt(HD)
 LOW = -1e30
 MESH = pl.DeviceIdType.MESH
@@ -124,6 +126,17 @@
     near = (-1, 1)
     halo = [d for k in range(REACH, 0, -1) for d in (-k, k)]
     blocks = [slice(b * BT, (b + 1) * BT) for b in range(BLOCKS)]
+    tp_device = {o: (s, at_tp(o)) for o in tp_far}
+    toward = jnp.where(2 * y >= n_y, 1, -1)
+    route = []
+    for step in (*range(REACH, 0, -1), *range(-REACH, 0)):
+        d = toward * step
+        there = at_chip(d)
+        devices = [(2 * there + h, tp) for h in range(2)]
+        route.append((REACH - d, devices))
+    beside = {d: (2 * at_chip(d) + core, tp) for d in halo}
+    slot_start = {d: (2 * (REACH - d) + core) * TOK for d in (0, *halo)}
+    tp_start = {o: at_tp(o) * cols for o in range(n_tp)}
     stage_a = [
         (2 * (z * n_y + lax.rem(y + oy, n_y)) + lax.rem(core + oc, 2), tp)
         for oy in range(n_y)
@@ -148,7 +161,7 @@
         ).start()
 
     barrier = pltpu.get_barrier_semaphore()
-    greeted = stage_a + stage_b
+    greeted = stage_b + stage_a
     for d in halo:
         for h in range(2):
             greeted.append((2 * at_chip(d) + h, tp))
@@ -184,7 +197,7 @@
                 xs.at[tp, pl.ds(b * BT, BT)],
                 sem_xs_s,
                 sem_xs_r.at[b],
-                (s, at_tp(o)),
+                tp_device[o],
             )
 
     def send_vector(n, b):
@@ -194,19 +207,15 @@
                 xg.at[n, tp, pl.ds(b * BT, BT)],
                 sem_xg_s.at[n],
                 sem_xg_r.at[n, b],
-                (s, at_tp(o)),
+                tp_device[o],
             )
-
-    def slot_rows(d, b):
-        start = (2 * (REACH - d) + core) * TOK + b * BT
-        return pl.ds(pl.multiple_of(start, BT), BT)
 
     def send_window(t, count, start, size, rsem):
         rows = pl.ds(start, size)
         place = pl.ds(t, count)
 
         def target(d):
-            first = (2 * (REACH - d) + core) * TOK + start
+            first = slot_start[d] + start
             return win.at[place, pl.ds(pl.multiple_of(first, BT), size)]
 
         send(qkv.at[other, place, rows], target(0), sem_q_s, rsem(REACH), pair)
@@ -242,7 +251,7 @@
                     win.at[pl.ds(t, count), pl.ds(first - d * CHIP, size)],
                     sem_q_s,
                     rsem(k - d),
-                    (2 * at_chip(d) + core, tp),
+                    beside[d],
                 )
 
     loading[2].wait()
@@ -291,32 +300,40 @@
             wait_kv(REACH - d, b)
         pass_on(1, 2, [b * BT, TOK + b * BT], BT, lambda k, b=b: sem_kv_r.at[k, b])
 
-    def send_grad_out(n, b, rows):
-        wait_for(xg.at[n, pl.ds(0, n_tp - 1), pl.ds(0, BT)], sem_xg_r.at[n, b])
-        acc = jnp.zeros((BT, 2 * HD), F32)
+    def send_grad_out(n, b):
+        rows = slice(b * GT, (b + 1) * GT)
+        for c in range(BLOCKS):
+            if b * GT <= c * BT < (b + 1) * GT:
+                wait_for(xg.at[n, pl.ds(0, n_tp - 1), pl.ds(0, BT)], sem_xg_r.at[n, c])
+        acc = jnp.zeros((GT, 2 * HD), F32)
         for r in range(n_tp):
             acc = acc + dot(xg[n, r, rows, :], w_o[:, r * cols : (r + 1) * cols], NT)
         acc = acc.astype(BF16)
         for h in range(2):
             g_msg[n, h, rows, :] = acc[:, h * HD : (h + 1) * HD]
-        taken = pl.ds(b * BT, BT)
+        taken = pl.ds(b * GT, GT)
+
+        def target(k):
+            first = (2 * k + core) * TOK + b * GT
+            return pl.ds(pl.multiple_of(first, GT), GT)
+
         send(
             g_msg.at[n, other, taken],
-            g_win.at[n, slot_rows(0, b)],
+            g_win.at[n, target(REACH)],
             sem_g_s.at[n],
             sem_g_r.at[n, REACH],
             pair,
         )
-        for d in halo:
+        for k, devices in route:
             for h in range(2):
                 send(
                     g_msg.at[n, h, taken],
-                    g_win.at[n, slot_rows(d, b)],
+                    g_win.at[n, target(k)],
                     sem_g_s.at[n],
-                    sem_g_r.at[n, REACH - d],
-                    (2 * at_chip(d) + h, tp),
+                    sem_g_r.at[n, k],
+                    devices[h],
                 )
-        g_win[n, slot_rows(0, b), :] = g_msg[n, core, rows, :]
+        g_win[n, target(REACH), :] = g_msg[n, core, rows, :]
 
     def send_corr(n):
         for h in range(2):
@@ -330,14 +347,14 @@
             sem_c_r.at[n, REACH],
             pair,
         )
-        for d in halo:
+        for k, devices in route:
             for h in range(2):
                 send(
                     c_msg.at[n, h],
-                    c_win.at[n, 2 * (REACH - d) + core],
+                    c_win.at[n, 2 * k + core],
                     sem_c_s.at[n],
-                    sem_c_r.at[n, REACH - d],
-                    (2 * at_chip(d) + h, tp),
+                    sem_c_r.at[n, k],
+                    devices[h],
                 )
         c_win[n, 2 * REACH + core] = c_msg[n, core]
 
@@ -359,6 +376,12 @@
     def part(k):
         return slice(k * CHIP, (k + 1) * CHIP)
 
+    def span(k):
+        return pl.ds(pl.multiple_of(k * CHIP, CHIP), CHIP)
+
+    soon = [REACH, *(REACH - toward * step for step in range(1, REACH + 1))]
+    last = [REACH + toward * step for step in range(1, REACH + 1)]
+
     def scores_of(k, peak):
         scores = dot(win[0, own, :], win[1, part(k), :], NT) * SCALE
         scores = jnp.where(valid(k), scores, LOW)
@@ -375,8 +398,8 @@
         wait_q(REACH - d)
     pass_on(0, 1, [0], CHIP, lambda k: sem_q_r.at[k])
     loading[8].wait()
-    for b, rows in enumerate(blocks):
-        send_grad_out(0, b, rows)
+    for b in range(GRAD_BLOCKS):
+        send_grad_out(0, b)
     for k in arrival[3:]:
         for b in range(BLOCKS):
             wait_kv(k, b)
@@ -402,7 +425,7 @@
             stats.at[REACH - d],
             sem_st_s,
             sem_st_r,
-            (2 * at_chip(d) + core, tp),
+            beside[d],
         )
     attended = jnp.zeros((CHIP, HD), F32)
     for k in arrival:
@@ -459,7 +482,7 @@
             return jnp.concatenate([g_full[n, 0, t], g_full[n, 1, t]], axis=1)
 
         def tp_rows(o):
-            return pl.ds(pl.multiple_of(at_tp(o) * cols, cols), cols)
+            return pl.ds(pl.multiple_of(tp_start[o], cols), cols)
 
         wait_for(g_win.at[n, pl.ds(0, TOK)], sem_g_r.at[n, REACH])
         grad = g_win[n, own, :]
@@ -478,20 +501,21 @@
             pair,
         )
         def key_side(k, values, wide, low):
-            grad = g_win[n, part(k), :]
+            grad = g_win[n, span(k), :]
             corr = jnp.concatenate([c_win[n, 2 * k], c_win[n, 2 * k + 1]], axis=1)
             score = (wide * (dot(values, grad, NT) - corr)).astype(BF16)
-            return dot(score, win[0, part(k), :], NN), dot(low, grad, NN)
+            return dot(score, win[0, span(k), :], NN), dot(low, grad, NN)
 
         def wait_grad(k):
-            if k != REACH:
+            mine = k is REACH
+            if not mine:
                 wait_for(g_win.at[n, pl.ds(0, CHIP)], sem_g_r.at[n, k])
-            wait_for(c_win.at[n, pl.ds(0, 1 if k == REACH else 2)], sem_c_r.at[n, k])
-
-        for place, k in enumerate(arrival[:3]):
+            wait_for(c_win.at[n, pl.ds(0, 1 if mine else 2)], sem_c_r.at[n, k])
+
+        for place, k in enumerate(soon):
             wait_grad(k)
             grad_k, grad_v = key_side(
-                k, win[2, own, :], probs_t[:, part(k)], probs_tb[:, part(k)]
+                k, win[2, own, :], probs_t[:, span(k)], probs_tb[:, span(k)]
             )
             if place == 0:
                 kv_acc[0] = grad_k
@@ -502,18 +526,18 @@
             else:
                 kv_acc[0] += grad_k
                 kv_acc[1] += grad_v
-        for k in arrival[3:]:
+        for k in last:
             wait_grad(k)
         for token_core in (other, core):
             taken = pl.ds(pl.multiple_of(token_core * TOK, TOK), TOK)
             window = pl.ds(pl.multiple_of(HALF + token_core * TOK, TOK), TOK)
             sums = [kv_acc[0, taken, :], kv_acc[1, taken, :]]
-            for k in arrival[3:]:
+            for k in last:
                 grad_k, grad_v = key_side(
                     k,
                     win[2, window, :],
-                    probs_t[taken, part(k)],
-                    probs_tb[taken, part(k)],
+                    probs_t[taken, span(k)],
+                    probs_tb[taken, span(k)],
                 )
                 sums = [sums[0] + grad_k, sums[1] + grad_v]
             for t in range(2):
@@ -544,7 +568,7 @@
                 rs_recv.at[n, o - 1, pl.ds(b * BT, BT)],
                 sem_rs_s.at[n],
                 sem_rs_r.at[n, b],
-                (s, at_tp(o)),
+                tp_device[o],
             )
 
         for o in tp_far:
@@ -574,8 +598,8 @@
 
         @pl.when(n < SSTEP - 1)
         def _():
-            for b, rows in enumerate(blocks):
-                send_grad_out(n + 1, b, rows)
+            for b in range(GRAD_BLOCKS):
+                send_grad_out(n + 1, b)
             send_corr(n + 1)
 
         for a in range(SSTEP):

time: 112 us -> 112 us (level)
  no operation moved by 1% of the time
where the time goes in v4:
time: 112 us
  Pallas kernels  110 us (98%)
  local copies, waits for them, and re-layouts  1.31 us (1%)
    pallas_call x1, Pallas kernels, on_device(): pl.pallas_call(functools.partial(kernel, sizes), out_shape=(pltpu.VMEM((t...  110 us

profile of v4, /device:TPU:1, one launch (start us, length us, event | category | flops | bytes accessed | tf_op | source)
XLA Modules:
  0.0 111.6 jit_solution(10872166857399371167)
XLA Ops:
  0.6 109.7 %block.1 = (f32[128,256]{1,0:T(8,128)S(1)}, f32[128,256]{1,0:T(8,128)S(1)}) custom-call(bf16[128,256]{1,0:T(8,128)(2,1)} %state.1, f32[128,256]{1,0:T(8,128)} %cot.1, f32[1,1024]{1,0:T(1,128)} %bitcast.1, bf16[1024,256]{1,0:T(8,128)(2,1)} %w_query.1, bf16[1024,256]{1,0:T(8,128)(2,1)} %w_key.1, bf16[1024,256]{1,0:T(8,128)(2,1)} %w_value.1, ...), custom_call_target="tpu_custom_call" | custom-call | tf_op jit(solution)/shard_map/block/pallas_call | solution.py:744
  110.3 0.7 copy.11
  111.0 0.7 copy.12

commit v5 on v4

--- a/solution.py
+++ b/solution.py
@@ -260,7 +260,7 @@
         if b == 0:
             loading[0].wait()
             loading[1].wait()
-        if b == BLOCKS - 1:
+        if b == 0:
             xg[0, tp] = kry[0].astype(BF16)
             for c in range(BLOCKS):
                 send_vector(0, c)
@@ -394,12 +394,12 @@
     peak = jnp.full((CHIP, 1), LOW, F32)
     for k in arrival[:3]:
         peak = scores_of(k, peak)
+    loading[8].wait()
+    for b in range(GRAD_BLOCKS):
+        send_grad_out(0, b)
     for d in near:
         wait_q(REACH - d)
     pass_on(0, 1, [0], CHIP, lambda k: sem_q_r.at[k])
-    loading[8].wait()
-    for b in range(GRAD_BLOCKS):
-        send_grad_out(0, b)
     for k in arrival[3:]:
         for b in range(BLOCKS):
             wait_kv(k, b)

time: 112 us -> 112 us (level)
  no operation moved by 1% of the time
where the time goes in v5:
time: 112 us
  Pallas kernels  110 us (98%)
  local copies, waits for them, and re-layouts  1.31 us (1%)
    pallas_call x1, Pallas kernels, on_device(): pl.pallas_call(functools.partial(kernel, sizes), out_shape=(pltpu.VMEM((t...  110 us

profile of v5, /device:TPU:1, one launch (start us, length us, event | category | flops | bytes accessed | tf_op | source)
XLA Modules:
  0.0 111.9 jit_solution(16201024740839018410)
XLA Ops:
  0.6 109.9 %block.1 = (f32[128,256]{1,0:T(8,128)S(1)}, f32[128,256]{1,0:T(8,128)S(1)}) custom-call(bf16[128,256]{1,0:T(8,128)(2,1)} %state.1, f32[128,256]{1,0:T(8,128)} %cot.1, f32[1,1024]{1,0:T(1,128)} %bitcast.1, bf16[1024,256]{1,0:T(8,128)(2,1)} %w_query.1, bf16[1024,256]{1,0:T(8,128)(2,1)} %w_key.1, bf16[1024,256]{1,0:T(8,128)(2,1)} %w_value.1, ...), custom_call_target="tpu_custom_call" | custom-call | tf_op jit(solution)/shard_map/block/pallas_call | solution.py:744
  110.5 0.7 copy.11
  111.2 0.7 copy.12
